TPU v7x, 128 devices: a whole 4x4x4 slice. The times are simulated.
128 devices in a mesh: node: 16 (over y, z), local: 8 (over x, core).
Axes of the slice: x: 4, y: 4, z: 4, core: 2. Of those that a mesh axis runs over, the one named last changes fastest.
Arguments:
- tokens: bfloat16 [16384, 2048], P(('node', 'local')), may hold values from -6 to 6
- grad_out: bfloat16 [16384, 2048], P(('node', 'local')), may hold values from -6 to 6
- gate_weights: float32 [16384, 2], P(('node', 'local')), may hold values from 0.2 to 1
- expert_ids: int32 [16384, 2], P(('node', 'local')), may hold values from 0 to 7, as said below
- slot_ids: int32 [16384, 2], P(('node', 'local')), may hold values from 0 to 16, as said below
- counts: int32 [128, 8], P(('node', 'local')), may hold values from 0 to 16, as said below
- w_in: bfloat16 [8, 2048, 8192], P('local', None, 'node'), may hold values from -0.125 to 0.125
- w_out: bfloat16 [8, 8192, 2048], P('local', 'node'), may hold values from -0.0625 to 0.0625
Outputs:
- grad_tokens: bfloat16 [16384, 2048], P(('node', 'local'))
- grad_w_in: float32 [8, 2048, 8192], P('local', None, 'node')
- grad_w_out: float32 [8, 8192, 2048], P('local', 'node')
Inputs may be any that keep to these rules, and one draw needn't show every extreme that they name: `expert_ids`: a token's two experts differ. slot_ids[t, k] is the number of earlier choices (in order of token, then k) on the same device naming the same expert, capped at 16. counts[d, e] is the number of choices on device d naming expert e, capped at 16.
All inputs are finite; a program needn't handle non-finite values.
Results may differ from a plain program's by a relative error of at most 0.0064.
Values may be sent and summed in bfloat16 or wider, within the bound.
A program may use at most 192 MiB of HBM per device.

v0:
```python
import jax
import jax.numpy as jnp
from jax import lax
from jax.sharding import PartitionSpec as P


def gelu_parts(values):
    cumulative = 0.5 * (1.0 + jax.scipy.special.erf(values * 0.7071067811865476))
    density = values * jnp.exp(-0.5 * values * values) * 0.3989422804014327
    return (values * cumulative, cumulative + density)


def body(tokens, grad_out, gate_weights, expert_ids, slot_ids, counts, w_in, w_out):
    experts = lax.axis_size("local")
    tok_rows = tokens.shape[0]
    model_width = tokens.shape[1]
    capacity = tok_rows // experts
    slot_rows = experts * capacity
    w_first = w_in[0]
    w_second = w_out[0]
    expert_range = jnp.arange(experts, dtype=jnp.int32)
    limits = jnp.sum(
        jnp.where(
            expert_ids[:, :, None] == expert_range[None, None, :], counts[0][None, None, :], 0
        ),
        axis=2,
    )
    is_kept = slot_ids < limits
    flat_index = jnp.where(is_kept, expert_ids * capacity + slot_ids, slot_rows)
    scaled = (gate_weights[:, :, None] * grad_out[:, None, :].astype(jnp.float32)).astype(
        jnp.bfloat16
    )
    repeated = jnp.broadcast_to(tokens[:, None, :], (tok_rows, 2, model_width)).reshape(
        -1, model_width
    )
    input_buffer = (
        jnp.zeros((slot_rows, model_width), jnp.bfloat16)
        .at[flat_index.reshape(-1)]
        .set(repeated, mode="drop")
    )
    grad_buffer = (
        jnp.zeros((slot_rows, model_width), jnp.bfloat16)
        .at[flat_index.reshape(-1)]
        .set(scaled.reshape(-1, model_width), mode="drop")
    )
    input_buffer = input_buffer.reshape(experts, capacity, model_width)
    grad_buffer = grad_buffer.reshape(experts, capacity, model_width)
    received = (
        lax.all_to_all(input_buffer, "local", split_axis=0, concat_axis=0, tiled=True),
        lax.all_to_all(grad_buffer, "local", split_axis=0, concat_axis=0, tiled=True),
    )
    input_piece = lax.all_gather(received[0][None], "node", axis=0, tiled=True)
    grad_piece = lax.all_gather(received[1][None], "node", axis=0, tiled=True)
    row_count = input_piece.shape[0] * input_piece.shape[1] * input_piece.shape[2]
    input_rows = input_piece.reshape(row_count, model_width)
    grad_rows = grad_piece.reshape(row_count, model_width)
    pre_act = jnp.dot(input_rows, w_first, preferred_element_type=jnp.float32)
    activated, slopes = gelu_parts(pre_act)
    hidden = activated.astype(jnp.bfloat16)
    back_hidden = lax.dot_general(
        grad_rows, w_second, (((1,), (1,)), ((), ())), preferred_element_type=jnp.float32
    )
    deltas = (back_hidden * slopes).astype(jnp.bfloat16)
    grad_second = lax.dot_general(
        hidden, grad_rows, (((0,), (0,)), ((), ())), preferred_element_type=jnp.float32
    )
    grad_first = lax.dot_general(
        input_rows, deltas, (((0,), (0,)), ((), ())), preferred_element_type=jnp.float32
    )
    grad_first, grad_second, all_deltas = (grad_first, grad_second, deltas)
    shares = lax.psum_scatter(
        lax.dot_general(
            all_deltas, w_first, (((1,), (1,)), ((), ())), preferred_element_type=jnp.float32
        ),
        "node",
        scatter_dimension=0,
        tiled=True,
    )
    shares = shares.astype(jnp.bfloat16).reshape(experts, capacity, model_width)
    returned = lax.all_to_all(shares, "local", split_axis=0, concat_axis=0, tiled=True)
    flat_rows = returned.reshape(slot_rows, model_width)
    picked = jnp.take(flat_rows, jnp.minimum(flat_index, slot_rows - 1).reshape(-1), axis=0).astype(
        jnp.float32
    )
    picked = picked.reshape(tok_rows, 2, model_width)
    picked = jnp.where(is_kept[:, :, None], picked, jnp.float32(0.0))
    grad_tokens = jnp.sum(picked, axis=1).astype(jnp.bfloat16)
    return (grad_tokens, grad_first[None], grad_second[None])


def solution(mesh):
    placed = (
        P(("node", "local"), None),
        P(("node", "local"), None),
        P(("node", "local"), None),
        P(("node", "local"), None),
        P(("node", "local"), None),
        P(("node", "local"), None),
        P("local", None, "node"),
        P("local", "node", None),
    )
    return jax.shard_map(
        body,
        mesh=mesh,
        in_specs=placed,
        out_specs=(P(("node", "local"), None), P("local", None, "node"), P("local", "node", None)),
        check_vma=False,
    )
```

profile of v0, /device:TPU:1, one launch (start us, length us, event | category | flops | bytes accessed | tf_op | source)
XLA Modules:
  0.0 337.0 jit_solution(6897836402594200744)
XLA Ops:
  7.2 0.0 copy-start
  7.2 0.0 copy-start.1
  7.2 0.0 all-gather.7.cloned.1.call-start
  7.2 0.9 select_reduce_fusion.1
  8.2 0.7 compare_and_fusion
  8.9 0.1 copy.28
  9.0 0.1 reshape.113
  9.1 1.7 broadcast_in_dim.72
  10.8 1.2 reshape.142
  12.0 2.9 scatter_custom_fusion.1
  14.9 15.1 %all_to_all.15 = bf16[8,16,2048]{2,1,0:T(8,128)(2,1)} all-to-all(bf16[8,16,2048]{2,1,0:T(8,128)(2,1)S(1)} %bitcast.30), channel_id=1, replica_groups=mesh['node'=16,'local'=8] {'local'}, dimensions={0} | all-to-all | bytes 1048576 | tf_op jit(solution)/shard_map/all_to_all | solution.py:49
  30.0 0.0 all-gather.7.cloned.1.call-update
  30.0 0.0 all-gather.5.cloned.1.call-start
  30.0 0.0 copy-done.1
  30.0 0.1 copy.29
  30.2 0.1 mul.62
  30.3 3.4 %mul.64 = f32[128,2,2048]{2,1,0:T(2,128)} broadcast(bf16[128,2048]{1,0:T(8,128)(2,1)} %param.9), dimensions={0,2} | broadcast | bytes 2621440 | tf_op jit(solution)/shard_map/mul | solution.py:30
  33.7 3.6 %mul.65 = f32[256,2048]{1,0:T(8,128)} reshape(f32[128,2,2048]{2,1,0:T(2,128)} %mul.64) | data formatting | bytes 4194304 | tf_op jit(solution)/shard_map/mul | solution.py:30
  37.4 3.3 scatter_custom_fusion
  40.7 13.5 %all_to_all.16 = bf16[8,16,2048]{2,1,0:T(8,128)(2,1)} all-to-all(bf16[8,16,2048]{2,1,0:T(8,128)(2,1)S(1)} %bitcast.31), channel_id=1, replica_groups=mesh['node'=16,'local'=8] {'local'}, dimensions={0} | all-to-all | bytes 1048576 | tf_op jit(solution)/shard_map/all_to_all | solution.py:50
  54.1 0.0 all-gather.5.cloned.1.call-update
  54.2 0.2 reduce-scatter.2.cloned.1.call-start
  54.4 47.5 %all-gather.7.cloned.1.call-done = bf16[128,16,2048]{2,1,0:T(8,128)(2,1)} async-done(((bf16[8,16,2048]{2,1,0:T(8,128)(2,1)}), bf16[128,16,2048]{2,1,0:T(8,128)(2,1)}) %all-gather.7.cloned.1.call-update) | async-done | bytes 8388624 | tf_op jit(solution)/shard_map/all_gather | solution.py:52
  101.9 0.0 copy-done
  101.9 9.5 %fusion.8 = f32[2048,512]{1,0:T(8,128)} fusion(bf16[2048,2048]{1,0:T(8,128)(2,1)} %bitcast.36, bf16[1,2048,512]{2,1,0:T(8,128)(2,1)S(1)} %copy-done), kind=kOutput, calls=%fused_computation.16 | convolution fusion | flops 4294967296 | bytes 14680064 | tf_op jit(solution)/shard_map/dot_general | solution.py:57
  111.5 63.1 %all-gather.5.cloned.1.call-done = bf16[128,16,2048]{2,1,0:T(8,128)(2,1)} async-done(((bf16[8,16,2048]{2,1,0:T(8,128)(2,1)}), bf16[128,16,2048]{2,1,0:T(8,128)(2,1)}) %all-gather.5.cloned.1.call-update) | async-done | bytes 8388624 | tf_op jit(solution)/shard_map/all_gather | solution.py:53
  174.5 9.3 %fusion.5 = bf16[2048,512]{1,0:T(8,128)(2,1)S(1)} fusion(f32[2048,512]{1,0:T(8,128)} %fusion.8, bf16[2048,2048]{1,0:T(8,128)(2,1)} %bitcast.38, bf16[1,512,2048]{2,1,0:T(8,128)(2,1)} %param.15), kind=kOutput, calls=%fused_computation.9 | convolution fusion | flops 4305453056 | bytes 16777216 | tf_op jit(solution)/shard_map/dot_general | solution.py:60
  183.8 0.0 copy-start.2
  183.8 1.3 copy-done.2
  185.1 8.3 %fusion.6 = f32[2048,2048]{1,0:T(8,128)} fusion(bf16[2048,512]{1,0:T(8,128)(2,1)S(1)} %fusion.5, bf16[1,2048,512]{2,1,0:T(8,128)(2,1)S(1)} %copy-done), kind=kOutput, calls=%fused_computation.14 | convolution fusion | flops 4294967296 | bytes 20971520 | tf_op jit(solution)/shard_map/dot_general | solution.py:72
  193.5 0.0 reduce-scatter.2.cloned.1.call-update
  193.5 0.1 copy.27
  193.6 0.1 copy.26
  193.8 0.1 copy.30
  193.9 0.1 reshape.121
  194.0 10.6 %convolution_bitcast_fusion.1 = f32[1,2048,512]{2,1,0:T(8,128)} fusion(bf16[2048,2048]{1,0:T(8,128)(2,1)} %bitcast.37, bf16[2048,512]{1,0:T(8,128)(2,1)} %copy-done.2), kind=kOutput, calls=%fused_computation.13 | convolution fusion | flops 4294967296 | bytes 14680064 | tf_op jit(solution)/shard_map/dot_general | solution.py:67
  204.6 98.9 %reduce-scatter.2.cloned.1.call-done = f32[128,2048]{1,0:T(8,128)} async-done(((f32[2048,2048]{1,0:T(8,128)}), f32[128,2048]{1,0:T(8,128)}) %reduce-scatter.2.cloned.1.call-update) | async-done | bytes 1048592 | tf_op jit(solution)/shard_map/reduce_scatter | solution.py:71
  303.5 2.1 convert_element_type.27
  305.6 5.4 %all-to-all-start.2 = ((bf16[8,16,2048]{2,1,0:T(8,128)(2,1)}), bf16[8,16,2048]{2,1,0:T(8,128)(2,1)S(1)}, u32[]{:S(2)}, u32[]{:S(2)}) async-start(bf16[8,16,2048]{2,1,0:T(8,128)(2,1)} %bitcast.8), calls=%async_computation.3 | async-start | bytes 1048576 | tf_op jit(solution)/shard_map/all_to_all | solution.py:80
  310.9 11.3 %convolution_bitcast_fusion = f32[1,512,2048]{2,1,0:T(8,128)} fusion(bf16[2048,2048]{1,0:T(8,128)(2,1)} %bitcast.39, f32[2048,512]{1,0:T(8,128)} %fusion.8), kind=kOutput, calls=%fused_computation.12 | convolution fusion | flops 4300210176 | bytes 16777216 | tf_op jit(solution)/shard_map/dot_general | solution.py:64
  322.3 0.0 all-to-all-done.2
  322.3 2.3 gather_fusion
  324.6 1.7 gather.7
  326.4 4.2 %select_reduce_fusion = bf16[128,2048]{1,0:T(8,128)(2,1)} fusion(pred[128,2]{1,0:T(8,128)(4,1)S(1)} %copy.26, bf16[128,2,2048]{2,1,0:T(2,128)(2,1)S(1)} %gather.7, pred[128,2]{1,0:T(8,128)(4,1)S(1)} %copy.27), kind=kLoop, calls=%fused_computation.19 | loop fusion | flops 1835008 | bytes 1573376 | tf_op jit(solution)/shard_map/reduce_sum | solution.py:87
  (4 shorter events, 0.0 us)
Async XLA Ops:
  7.2 94.8 %copy-start = (bf16[1,2048,512]{2,1,0:T(8,128)(2,1)S(1)}, bf16[1,2048,512]{2,1,0:T(8,128)(2,1)}, u32[]{:S(2)}) copy-start(bf16[1,2048,512]{2,1,0:T(8,128)(2,1)} %param.14) | copy-start | bytes 6291460
  7.2 22.9 %copy-start.1 = (f32[128,2]{0,1:T(2,128)S(1)}, f32[128,2]{0,1:T(2,128)}, u32[]{:S(2)}) copy-start(f32[128,2]{0,1:T(2,128)} %param.10) | copy-start | bytes 3076
  7.2 94.7 %all-gather.7.cloned.1.call-start = ((), (), s32[]{:S(2)}) async-start(), calls=%async_computation.6 | async-start | bytes 8912896 | tf_op jit(solution)/shard_map/all_gather | solution.py:52
  30.0 144.6 %all-gather.5.cloned.1.call-start = ((), (), s32[]{:S(2)}) async-start(), calls=%async_computation.5 | async-start | bytes 8912896 | tf_op jit(solution)/shard_map/all_gather | solution.py:53
  54.2 249.3 %reduce-scatter.2.cloned.1.call-start = ((), (), s32[]{:S(2)}) async-start(), calls=%async_computation.4 | async-start | bytes 17825792 | tf_op jit(solution)/shard_map/reduce_scatter | solution.py:71
  183.8 1.3 copy-start.2
  305.6 16.7 %all-to-all-start.2 = ((bf16[8,16,2048]{2,1,0:T(8,128)(2,1)}), bf16[8,16,2048]{2,1,0:T(8,128)(2,1)S(1)}, u32[]{:S(2)}, u32[]{:S(2)}) async-start(bf16[8,16,2048]{2,1,0:T(8,128)(2,1)} %bitcast.8), calls=%async_computation.3 | async-start | bytes 1048576 | tf_op jit(solution)/shard_map/all_to_all | solution.py:80
Sparse Core Ops, SparseCore 0:
  30.1 71.7 all-gather.6
  104.1 70.4 all-gather.4
  193.6 109.8 reduce-scatter.1
where the time goes:
time: 338 us; the launch traced here: 337 us
  waiting for transfers between devices  210 us (62%)
  matrix products  49 us (14%)
  blocking collectives  28.5 us (8%)
  local copies, waits for them, and re-layouts  19.3 us (6%)
  between operations  13.9 us (4%)
  other arithmetic  11.2 us (3%)
  starting transfers between devices  5.67 us (2%)
    reduce_scatter x1, waiting for transfers between devices, body(): lax.psum_scatter(lax.dot_general(all_deltas, w_first, (((1,), (1,)), ((),...  98.9 us
    all_gather x1, waiting for transfers between devices, body(): grad_piece = lax.all_gather(received[1][None], 'node', axis=0, tiled=True)  63.1 us
    all_gather x1, waiting for transfers between devices, body(): input_piece = lax.all_gather(received[0][None], 'node', axis=0, tiled=True)  47.5 us
    all_to_all x1, blocking collectives, body(): lax.all_to_all(input_buffer, 'local', split_axis=0, concat_axis=0, tiled=...  15.1 us
    all_to_all x1, blocking collectives, body(): lax.all_to_all(grad_buffer, 'local', split_axis=0, concat_axis=0, tiled=T...  13.5 us
    dot_general x1, matrix products, body(): lax.dot_general(hidden, grad_rows, (((0,), (0,)), ((), ())), preferred_el...  11.3 us
    dot_general x1, matrix products, body(): lax.dot_general(input_rows, deltas, (((0,), (0,)), ((), ())), preferred_e...  10.6 us
    dot_general x1, matrix products, body(): pre_act = jnp.dot(input_rows, w_first, preferred_element_type=jnp.float32)  9.53 us
  transfers between devices with their start and end apart: 4, of which 3 were waited for; matrix products, arithmetic and copies ran while one was open for 13% of the time, Pallas kernels for 0%

commit v1 on v0

v1 whole, which is shorter than its diff:
```python
import functools

import jax
import jax.numpy as jnp
from jax import lax
from jax.experimental import pallas as pl
from jax.experimental.pallas import tpu as pltpu
from jax.sharding import PartitionSpec as P

MESH = pl.DeviceIdType.MESH
BF16 = jnp.bfloat16
F32 = jnp.float32

SIDE = 4
CORES = 2
EXPERTS = 8
CAP = 16
NODES = SIDE * SIDE
CHUNKS = SIDE
DX = (0, 1, 3, 2)
RETURN_ORDER = (1, 2, 3, 0)
PART = NODES * CAP
CHUNK = CORES * PART
COLUMN = SIDE * CAP


def gelu_parts(values):
    cumulative = 0.5 * (1.0 + lax.erf(values * 0.7071067811865476))
    density = values * jnp.exp(-0.5 * values * values) * 0.3989422804014327
    return (values * cumulative, cumulative + density)


def turn(value, step):
    return lax.rem(value + step, SIDE)


def kernel(
    tokens, grad_out, gates, ids, slots, counts, w_in, w_out,
    grad_tokens, grad_in, grad_second,
    rows, w1, w2, back, acc_in, acc_out, acc_turned, out_x, out_g, returned, held,
    hidden_t, delta, delta_t, slopes, relay, arrived, relay_block, arrived_block, final,
    load_sem, store_sem, swap_send, swap_recv, gather_send, gather_recv,
    sum_send, sum_recv, home_send, home_recv,
):
    width = rows.shape[1]
    half = width // 2
    units = w2.shape[0]
    node, local = lax.axis_index("node"), lax.axis_index("local")
    y, z = node // SIDE, lax.rem(node, SIDE)
    x, core = local // CORES, lax.rem(local, CORES)

    primary, secondary = (y, z), (z, y)

    def at(part, a, b):
        return a * SIDE + b if part == 0 else b * SIDE + a

    def on_primary(part, step):
        return (at(part, turn(primary[part], step), secondary[part]), local)

    def on_secondary(part, step):
        return (at(part, primary[part], turn(secondary[part], step)), local)

    def block(part, da, db):
        return turn(secondary[part], db) * SIDE + turn(primary[part], da)

    def spot(k, g, part, place):
        return pl.ds(pl.multiple_of(((k * 2 + g) * 2 + part) * PART + place * CAP, CAP), CAP)

    def drain(ref, count, sem):
        view = ref.at[pl.ds(0, count)]
        pltpu.make_async_copy(view, view, sem).wait()

    def push(src, dst, send, recv, device):
        pltpu.make_async_remote_copy(
            src_ref=src, dst_ref=dst, send_sem=send, recv_sem=recv,
            device_id=device, device_id_type=MESH,
        ).start()

    barrier = pltpu.get_barrier_semaphore()
    partners = [on_primary(0, 1), on_primary(0, 3), on_primary(1, 1), on_primary(1, 3)]
    for dx in range(SIDE):
        for flip in range(CORES):
            if dx or flip:
                partners.append((node, turn(x, dx) * CORES + lax.rem(core + flip, CORES)))
    for partner in partners:
        pl.semaphore_signal(barrier, inc=1, device_id=partner, device_id_type=MESH)

    first_load = pltpu.make_async_copy(w_in.at[0], w1, load_sem.at[0])
    second_load = pltpu.make_async_copy(w_out.at[0], w2, load_sem.at[1])
    first_load.start()
    second_load.start()

    limits = counts[...].astype(F32)
    expert_lanes = lax.broadcasted_iota(jnp.int32, (ids.shape[0], EXPERTS), 1)
    slot_lanes = lax.broadcasted_iota(jnp.int32, (ids.shape[0], EXPERTS * CAP), 1)
    picks, weighted = None, None
    for choice in range(2):
        expert = ids[:, choice : choice + 1]
        slot = slots[:, choice : choice + 1]
        limit = jnp.sum(
            jnp.where(expert == expert_lanes, limits, 0.0), axis=1, keepdims=True
        )
        place = jnp.where(slot.astype(F32) < limit, expert * CAP + slot, -1)
        pick = jnp.where(place == slot_lanes, 1.0, 0.0)
        scale = pick * gates[:, choice : choice + 1]
        picks = pick if picks is None else picks + pick
        weighted = scale if weighted is None else weighted + scale
    held[...] = picks.astype(BF16)
    to_slots = picks.T.astype(BF16)
    slot_gate = jnp.sum(weighted.T, axis=1, keepdims=True)
    out_x[...] = jnp.dot(to_slots, tokens[...], preferred_element_type=F32).astype(BF16)
    out_g[...] = (
        slot_gate * jnp.dot(to_slots, grad_out[...], preferred_element_type=F32)
    ).astype(BF16)
    own = pl.ds(pl.multiple_of(local * CAP, CAP), CAP)
    for part in range(CORES):

        @pl.when(core == part)
        def _():
            rows[spot(0, 0, part, block(part, 0, 0)), :] = out_x[own, :]
            rows[spot(0, 1, part, block(part, 0, 0)), :] = out_g[own, :]

    pl.semaphore_wait(barrier, len(partners))

    for k in range(CHUNKS):
        for flip in range(CORES):
            if k or flip:
                target = turn(x, SIDE - DX[k]) * CORES + lax.rem(core + flip, CORES)
                there = pl.ds(pl.multiple_of(target * CAP, CAP), CAP)
                mine = jnp.where(core == 0, block(0, 0, 0), block(1, 0, 0))
                for g, source in enumerate((out_x, out_g)):
                    push(
                        source.at[there], rows.at[spot(k, g, core, mine)],
                        swap_send, swap_recv.at[k, core], (node, target),
                    )

    acc_in[...] = jnp.zeros_like(acc_in)
    acc_out[...] = jnp.zeros_like(acc_out)

    def ship(k, g, part, place, device, event):
        where = rows.at[spot(k, g, part, place)]
        push(where, where, gather_send.at[k], gather_recv.at[k, part, event], device)

    def gather_start(k, first=False):
        for part in range(CORES):
            if first:
                pl.when(core != part)(lambda: drain(rows, 2 * CAP, swap_recv.at[k, part]))
            else:
                drain(rows, 2 * CAP, swap_recv.at[k, part])
            for g in range(2):
                mine = block(part, 0, 0)
                ship(k, g, part, mine, on_primary(part, 1), 0)
                ship(k, g, part, mine, on_primary(part, 3), 1)
            for g in range(2):
                ship(k, g, part, mine, on_secondary(part, 1), 3)
                ship(k, g, part, mine, on_secondary(part, 3), 4)

    def gather_near(k):
        for part in range(CORES):
            drain(rows, 2 * CAP, gather_recv.at[k, part, 0])
            ship(k, 0, part, block(part, 3, 0), on_primary(part, 1), 2)
            drain(rows, 2 * CAP, gather_recv.at[k, part, 1])
            ship(k, 1, part, block(part, 1, 0), on_primary(part, 3), 2)
        for part in range(CORES):
            for da in (3, 1):
                for g in range(2):
                    ship(k, g, part, block(part, da, 0), on_secondary(part, 1), 5)
                    ship(k, g, part, block(part, da, 0), on_secondary(part, 3), 6)

    def gather_far(k):
        for part in range(CORES):
            drain(rows, 2 * CAP, gather_recv.at[k, part, 2])
            for g in range(2):
                ship(k, g, part, block(part, 2, 0), on_secondary(part, 1), 7)
                ship(k, g, part, block(part, 2, 0), on_secondary(part, 3), 8)

    def gather_pass(k, event, steps):
        for part in range(CORES):
            drain(rows, 2 * len(steps) * CAP, gather_recv.at[k, part, event])
            for da in steps:
                ship(k, 0, part, block(part, da, 3), on_secondary(part, 1), 9)
            drain(rows, 2 * len(steps) * CAP, gather_recv.at[k, part, event + 1])
            for da in steps:
                ship(k, 1, part, block(part, da, 1), on_secondary(part, 3), 9)

    def gather_end(k):
        for part in range(CORES):
            drain(rows, 2 * SIDE * CAP, gather_recv.at[k, part, 9])

    def section(k, g, part):
        start = ((k * 2 + g) * 2 + part) * PART
        return pl.ds(pl.multiple_of(start, PART), PART)

    def activate(k, part):
        pre = jnp.dot(rows[section(k, 0, part), :], w1[...], preferred_element_type=F32)
        activated, slope = gelu_parts(pre)
        hidden_t[:, part * PART : (part + 1) * PART] = activated.T.astype(BF16)
        slopes[part * PART : (part + 1) * PART, :] = slope

    def backward(k, part):
        span = slice(part * PART, (part + 1) * PART)
        back_hidden = lax.dot_general(
            rows[section(k, 1, part), :], w2[...], (((1,), (1,)), ((), ())),
            preferred_element_type=F32,
        )
        change = back_hidden * slopes[span, :]
        delta[span, :] = change.astype(BF16)
        delta_t[:, span] = change.T.astype(BF16)

    def to_inputs(k, part):
        span = slice(part * PART, (part + 1) * PART)
        for start in range(0, width, units):
            back[
                pl.ds(pl.multiple_of(k * CHUNK + part * PART, PART), PART), start : start + units
            ] = lax.dot_general(
                delta[span, :], w1[start : start + units, :], (((1,), (1,)), ((), ())),
                preferred_element_type=F32,
            ).astype(BF16)

    def to_weights(k, g, left, total, start):
        span = pl.ds(pl.multiple_of((k * 2 + g) * CHUNK, CHUNK), CHUNK)
        total[:, start : start + units] += jnp.dot(
            left[...], rows[span, start : start + units], preferred_element_type=F32
        )

    def pieces(k):
        done = []
        for part in range(CORES):
            done.append(functools.partial(activate, k, part))
        for part in range(CORES):
            done.append(functools.partial(backward, k, part))
        for part in range(CORES):
            done.append(functools.partial(to_inputs, k, part))
        for g, left, total in ((1, hidden_t, acc_out), (0, delta_t, acc_in)):
            for start in range(0, width, units):
                done.append(functools.partial(to_weights, k, g, left, total, start))
        return done

    def run(work, count):
        for _ in range(min(count, len(work))):
            work.pop(0)()

    gather_start(0, first=True)
    first_load.wait()
    second_load.wait()

    @pl.loop(0, CHUNKS)
    def _(k):
        def compute(count):
            @pl.when(k > 0)
            def _():
                run(work, count)

        work = pieces(k - 1)
        gather_near(k)
        compute(3)
        gather_pass(k, 3, (0,))
        compute(2)
        gather_far(k)

        @pl.when(k < CHUNKS - 1)
        def _():
            gather_start(k + 1)

        compute(3)
        gather_pass(k, 5, (3, 1))
        compute(3)
        gather_pass(k, 7, (2,))
        compute(3)
        gather_end(k)

    def strip(k, part, db, low, high):
        start = k * CHUNK + part * PART + turn(secondary[part], db) * COLUMN + low
        return pl.ds(pl.multiple_of(start, CAP), high - low)

    middle = COLUMN // 2

    def column_start(k):
        for part in range(CORES):
            for side, step in ((0, 1), (1, 3)):
                low, high = ((0, middle), (middle, COLUMN))[side]
                push(
                    back.at[strip(k, part, 2, low, high)], relay.at[k, part, side],
                    sum_send.at[k], sum_recv.at[k, part, side], on_secondary(part, step),
                )
            for side, step in ((0, 1), (1, 3)):
                low, high = ((middle, COLUMN), (0, middle))[side]
                push(
                    back.at[strip(k, part, step, low, high)],
                    arrived.at[k, part, side, pl.ds(low, middle)],
                    sum_send.at[k], sum_recv.at[k, part, 2 + side], on_secondary(part, step),
                )

    def column_pass(k):
        for part in range(CORES):
            for side, step in ((0, 1), (1, 3)):
                low, high = ((0, middle), (middle, COLUMN))[side]
                where = strip(k, part, step, low, high)
                drain(back, middle, sum_recv.at[k, part, side])
                back[where, :] = (
                    back[where, :].astype(F32) + relay[k, part, side].astype(F32)
                ).astype(BF16)
                push(
                    back.at[where], arrived.at[k, part, side, pl.ds(low, middle)],
                    sum_send.at[k], sum_recv.at[k, part, 2 + side], on_secondary(part, step),
                )

    def lump(k, part, da):
        start = k * CHUNK + part * PART + block(part, da, 0) * CAP
        return pl.ds(pl.multiple_of(start, CAP), CAP)

    lanes = (pl.ds(0, half), pl.ds(half, half))

    def column_end(k):
        for part in range(CORES):
            drain(back, COLUMN, sum_recv.at[k, part, 2])
            drain(back, COLUMN, sum_recv.at[k, part, 3])
            where = strip(k, part, 0, 0, COLUMN)
            back[where, :] = (
                back[where, :].astype(F32)
                + arrived[k, part, 0].astype(F32)
                + arrived[k, part, 1].astype(F32)
            ).astype(BF16)
            for side, step in ((0, 1), (1, 3)):
                push(
                    back.at[lump(k, part, 2), lanes[side]], relay_block.at[k, part, side],
                    sum_send.at[k], sum_recv.at[k, part, 4 + side], on_primary(part, step),
                )
            for side, step in ((0, 1), (1, 3)):
                push(
                    back.at[lump(k, part, step), lanes[1 - side]],
                    arrived_block.at[k, part, side, :, lanes[1 - side]],
                    sum_send.at[k], sum_recv.at[k, part, 6 + side], on_primary(part, step),
                )

    def block_pass(k):
        for part in range(CORES):
            for side, step in ((0, 1), (1, 3)):
                where = lump(k, part, step)
                pltpu.make_async_copy(
                    relay_block.at[k, part, side], relay_block.at[k, part, side],
                    sum_recv.at[k, part, 4 + side],
                ).wait()
                back[where, lanes[side]] = (
                    back[where, lanes[side]].astype(F32) + relay_block[k, part, side].astype(F32)
                ).astype(BF16)
                push(
                    back.at[where, lanes[side]], arrived_block.at[k, part, side, :, lanes[side]],
                    sum_send.at[k], sum_recv.at[k, part, 6 + side], on_primary(part, step),
                )

    def block_end(k):
        for part in range(CORES):
            drain(back, CAP, sum_recv.at[k, part, 6])
            drain(back, CAP, sum_recv.at[k, part, 7])
            total = (
                back[lump(k, part, 0), :].astype(F32)
                + arrived_block[k, part, 0].astype(F32)
                + arrived_block[k, part, 1].astype(F32)
            ).astype(BF16)
            target = (node, turn(x, DX[k]) * CORES + part)

            def keep():
                returned[own, :] = total

            def send():
                final[k, part] = total
                push(
                    final.at[k, part], returned.at[own],
                    home_send, home_recv.at[k, core], target,
                )

            if k == 0:
                pl.when(core == part)(keep)
                pl.when(core != part)(send)
            else:
                send()

    work = pieces(CHUNKS - 1)
    r0, r1, r2, r3 = RETURN_ORDER
    column_start(r0)
    column_start(r1)
    run(work, 2)
    column_pass(r0)
    run(work, 2)
    column_pass(r1)
    run(work, 2)
    column_end(r0)
    column_start(r2)
    run(work, 2)
    column_end(r1)
    block_pass(r0)
    run(work, 2)
    column_pass(r2)
    column_start(r3)
    run(work, 2)
    block_end(r0)
    block_pass(r1)
    run(work, 2)
    first_store = pltpu.make_async_copy(acc_out, grad_second.at[0], store_sem.at[0])
    first_store.start()
    column_end(r2)
    column_pass(r3)
    block_end(r1)
    block_pass(r2)
    for start in range(0, width, units):
        acc_turned[start : start + units, :] = acc_in[:, start : start + units].T
    second_store = pltpu.make_async_copy(acc_turned, grad_in.at[0], store_sem.at[1])
    second_store.start()
    column_end(r3)
    block_end(r2)
    block_pass(r3)
    block_end(r3)

    for k in range(CHUNKS):
        for part in range(CORES):
            if k:
                drain(back, CAP, home_recv.at[k, part])
            else:
                pl.when(core != part)(lambda: drain(back, CAP, home_recv.at[k, part]))
    grad_tokens[...] = jnp.dot(
        held[...], returned[...], preferred_element_type=F32
    ).astype(BF16)

    first_store.wait()
    second_store.wait()
    drain(rows, 2 * (EXPERTS - 1) * CAP, swap_send)
    drain(rows, (EXPERTS - 1) * CAP, home_send)
    for k in range(CHUNKS):
        drain(rows, CORES * 30 * CAP, gather_send.at[k])
        drain(rows, CORES * 15 * CAP, sum_send.at[k])


def body(tokens, grad_out, gate_weights, expert_ids, slot_ids, counts, w_in, w_out):
    token_rows, width = tokens.shape
    units = w_out.shape[1]
    in_vmem = pl.BlockSpec(memory_space=pltpu.VMEM)
    in_hbm = pl.BlockSpec(memory_space=pl.ANY)
    dma = pltpu.SemaphoreType.DMA
    return pl.pallas_call(
        kernel,
        out_shape=(
            jax.ShapeDtypeStruct(tokens.shape, BF16),
            jax.ShapeDtypeStruct(w_in.shape, F32),
            jax.ShapeDtypeStruct(w_out.shape, F32),
        ),
        in_specs=[in_vmem] * 6 + [in_hbm] * 2,
        out_specs=(in_vmem, in_hbm, in_hbm),
        scratch_shapes=[
            pltpu.VMEM((CHUNKS * 2 * CHUNK, width), BF16),
            pltpu.VMEM((width, units), BF16),
            pltpu.VMEM((units, width), BF16),
            pltpu.VMEM((CHUNKS * CHUNK, width), BF16),
            pltpu.VMEM((units, width), F32),
            pltpu.VMEM((units, width), F32),
            pltpu.VMEM((width, units), F32),
            pltpu.VMEM((EXPERTS * CAP, width), BF16),
            pltpu.VMEM((EXPERTS * CAP, width), BF16),
            pltpu.VMEM((EXPERTS * CAP, width), BF16),
            pltpu.VMEM((token_rows, EXPERTS * CAP), BF16),
            pltpu.VMEM((units, CHUNK), BF16),
            pltpu.VMEM((CHUNK, units), BF16),
            pltpu.VMEM((units, CHUNK), BF16),
            pltpu.VMEM((CHUNK, units), F32),
            pltpu.VMEM((CHUNKS, CORES, 2, COLUMN // 2, width), BF16),
            pltpu.VMEM((CHUNKS, CORES, 2, COLUMN, width), BF16),
            pltpu.VMEM((CHUNKS, CORES, 2, CAP, width // 2), BF16),
            pltpu.VMEM((CHUNKS, CORES, 2, CAP, width), BF16),
            pltpu.VMEM((CHUNKS, CORES, CAP, width), BF16),
            dma((2,)),
            dma((2,)),
            dma,
            dma((CHUNKS, CORES)),
            dma((CHUNKS,)),
            dma((CHUNKS, CORES, 10)),
            dma((CHUNKS,)),
            dma((CHUNKS, CORES, 8)),
            dma,
            dma((CHUNKS, CORES)),
        ],
        compiler_params=pltpu.CompilerParams(
            collective_id=0, has_side_effects=True, vmem_limit_bytes=62 * 2**20
        ),
        cost_estimate=pl.CostEstimate(
            flops=10 * NODES * EXPERTS * CAP * width * units,
            bytes_accessed=16 * width * units,
            transcendentals=0,
        ),
    )(tokens, grad_out, gate_weights, expert_ids, slot_ids, counts, w_in, w_out)


def solution(mesh):
    placed = (
        P(("node", "local"), None),
        P(("node", "local"), None),
        P(("node", "local"), None),
        P(("node", "local"), None),
        P(("node", "local"), None),
        P(("node", "local"), None),
        P("local", None, "node"),
        P("local", "node", None),
    )
    return jax.shard_map(
        body,
        mesh=mesh,
        in_specs=placed,
        out_specs=(P(("node", "local"), None), P("local", None, "node"), P("local", "node", None)),
        check_vma=False,
    )
```

time: 338 us -> 171 us (0.51)
  waiting for transfers between devices: 210 us -> 0 us
  Pallas kernels: 0 us -> 157 us
  matrix products: 49 us -> 0 us
  blocking collectives: 28.5 us -> 0 us
  between operations: 13.9 us -> 0.64 us
  other arithmetic: 11.2 us -> 0 us
  local copies, waits for them, and re-layouts: 19.3 us -> 13 us
  starting transfers between devices: 5.67 us -> 0 us
    pallas_call x0 -> x1, Pallas kernels: none -> 157 us  [body(): pl.pallas_call(kernel, out_shape=(jax.ShapeDtypeStruct(tokens.shape, BF16...]
    all_gather x2 -> x0, waiting for transfers between devices: 111 us -> none  [the longest x1 63.1 us: body(): grad_piece = lax.all_gather(received[1][None], 'node', axis=0, tiled=True)]
    reduce_scatter x1 -> x0, waiting for transfers between devices: 98.9 us -> none  [body(): lax.psum_scatter(lax.dot_general(all_deltas, w_first, (((1,), (1,)), ((),...]
    dot_general x5 -> x0, matrix products: 49 us -> none  [the longest x1 11.3 us: body(): lax.dot_general(hidden, grad_rows, (((0,), (0,)), ((), ())), preferred_el...]
    all_to_all x2 -> x0, blocking collectives: 28.5 us -> none  [the longest x1 15.1 us: body(): lax.all_to_all(input_buffer, 'local', split_axis=0, concat_axis=0, tiled=...]
    unnamed x7 -> x8, local copies, waits for them, and re-layouts: 1.44 us -> 13 us
    mul x3 -> x0, local copies, waits for them, and re-layouts: 7.2 us -> none  [body(): gate_weights[:, :, None] * grad_out[:, None, :].astype(jnp.float32)]
    all_to_all x1 -> x0, starting transfers between devices: 5.37 us -> none  [body(): lax.all_to_all(shares, 'local', split_axis=0, concat_axis=0, tiled=True)]
  transfers between devices with their start and end apart: 4 -> 0, of which waited for: 3 -> 0; matrix products, arithmetic and copies ran while one was open for 13% -> 0% of each run, Pallas kernels for 0% -> 0%
where the time goes in v1:
time: 171 us; the launch traced here: 170 us
  Pallas kernels  157 us (92%)
  local copies, waits for them, and re-layouts  13 us (8%)
    pallas_call x1, Pallas kernels, body(): pl.pallas_call(kernel, out_shape=(jax.ShapeDtypeStruct(tokens.shape, BF16...  157 us
    unnamed x8, local copies, waits for them, and re-layouts  13 us

profile of v1, /device:TPU:1, one launch (start us, length us, event | category | flops | bytes accessed | tf_op | source)
XLA Modules:
  0.0 170.5 jit_solution(1809368194766580759)
XLA Ops:
  0.6 1.4 copy.11.gates
  2.0 1.4 copy.12.ids
  3.5 1.4 copy.13.slots
  4.9 156.9 %shard_map.103 = (bf16[128,2048]{1,0:T(8,128)(2,1)}, f32[1,2048,512]{2,1,0:T(8,128)}, f32[1,512,2048]{2,1,0:T(8,128)}) custom-call(bf16[128,2048]{1,0:T(8,128)(2,1)} %tokens.1, bf16[128,2048]{1,0:T(8,128)(2,1)} %grad_out.1, f32[128,2]{1,0:T(8,128)} %copy.11.gates, s32[128,2]{1,0:T(8,128)} %copy.12.ids, s32[128,2]{1,0:T(8,128)} %copy.13.slots, ...), custom_call_target="tpu_custom_call" | custom-call | flops 21474836480 | bytes 16777216 | tf_op jit(solution)/shard_map/pallas_call | solution.py:440
  161.8 1.9 %copy.17 = bf16[128,2048]{1,0:T(8,128)(2,1)} copy(bf16[128,2048]{1,0:T(8,128)(2,1)} %get-tuple-element.6) | data formatting | bytes 1048576
  163.6 0.0 copy-start
  163.6 4.8 %copy.18 = f32[1,2048,512]{2,1,0:T(8,128)} copy(f32[1,2048,512]{2,1,0:T(8,128)} %get-tuple-element.7) | data formatting | bytes 8388608
  168.5 0.0 copy-done
  168.5 2.0 %copy.19 = f32[1,512,2048]{2,1,0:T(8,128)} copy(f32[1,512,2048]{2,1,0:T(8,128)S(1)} %copy-done) | data formatting | bytes 8388608
Async XLA Ops:
  163.6 4.8 %copy-start = (f32[1,512,2048]{2,1,0:T(8,128)S(1)}, f32[1,512,2048]{2,1,0:T(8,128)}, u32[]{:S(2)}) copy-start(f32[1,512,2048]{2,1,0:T(8,128)} %get-tuple-element.8) | copy-start | bytes 12582916

commit v2 on v1

--- a/solution.py
+++ b/solution.py
@@ -17,8 +17,9 @@
 CAP = 16
 NODES = SIDE * SIDE
 CHUNKS = SIDE
-DX = (0, 1, 3, 2)
-RETURN_ORDER = (1, 2, 3, 0)
+DX = (0, 1, 2, 3)
+RETURN_ORDER = (1, 2, 0, 3)
+PIECES = 4
 PART = NODES * CAP
 CHUNK = CORES * PART
 COLUMN = SIDE * CAP
@@ -36,9 +37,9 @@
 
 def kernel(
     tokens, grad_out, gates, ids, slots, counts, w_in, w_out,
-    grad_tokens, grad_in, grad_second,
-    rows, w1, w2, back, acc_in, acc_out, acc_turned, out_x, out_g, returned, held,
-    hidden_t, delta, delta_t, slopes, relay, arrived, relay_block, arrived_block, final,
+    picked_out, returned_out, grad_in, grad_second,
+    rows, w1, w2, back, turned, rounded, out_x, out_g, returned, held,
+    hidden_t, delta, delta_t, slopes, relay, arrived, relay_block, arrived_block, across, final,
     load_sem, store_sem, swap_send, swap_recv, gather_send, gather_recv,
     sum_send, sum_recv, home_send, home_recv,
 ):
@@ -77,7 +78,7 @@
         ).start()
 
     barrier = pltpu.get_barrier_semaphore()
-    partners = [on_primary(0, 1), on_primary(0, 3), on_primary(1, 1), on_primary(1, 3)]
+    partners = [on_primary(part, step) for part in range(CORES) for step in (1, 2, 3)]
     for dx in range(SIDE):
         for flip in range(CORES):
             if dx or flip:
@@ -91,18 +92,21 @@
     second_load.start()
 
     limits = counts[...].astype(F32)
-    expert_lanes = lax.broadcasted_iota(jnp.int32, (ids.shape[0], EXPERTS), 1)
-    slot_lanes = lax.broadcasted_iota(jnp.int32, (ids.shape[0], EXPERTS * CAP), 1)
+    expert_lanes = lax.broadcasted_iota(jnp.int32, (ids.shape[1], EXPERTS), 1)
+    slot_lanes = lax.broadcasted_iota(jnp.int32, (ids.shape[1], EXPERTS * CAP), 1)
     picks, weighted = None, None
+    ids_down, slots_down, gates_down = (
+        jnp.concatenate([ref[...].astype(F32)] * 4, axis=0).T for ref in (ids, slots, gates)
+    )
     for choice in range(2):
-        expert = ids[:, choice : choice + 1]
-        slot = slots[:, choice : choice + 1]
+        expert = ids_down[:, choice : choice + 1].astype(jnp.int32)
+        slot = slots_down[:, choice : choice + 1].astype(jnp.int32)
         limit = jnp.sum(
             jnp.where(expert == expert_lanes, limits, 0.0), axis=1, keepdims=True
         )
         place = jnp.where(slot.astype(F32) < limit, expert * CAP + slot, -1)
         pick = jnp.where(place == slot_lanes, 1.0, 0.0)
-        scale = pick * gates[:, choice : choice + 1]
+        scale = pick * gates_down[:, choice : choice + 1]
         picks = pick if picks is None else picks + pick
         weighted = scale if weighted is None else weighted + scale
     held[...] = picks.astype(BF16)
@@ -122,38 +126,33 @@
 
     pl.semaphore_wait(barrier, len(partners))
 
-    for k in range(CHUNKS):
-        for flip in range(CORES):
-            if k or flip:
-                target = turn(x, SIDE - DX[k]) * CORES + lax.rem(core + flip, CORES)
-                there = pl.ds(pl.multiple_of(target * CAP, CAP), CAP)
-                mine = jnp.where(core == 0, block(0, 0, 0), block(1, 0, 0))
-                for g, source in enumerate((out_x, out_g)):
-                    push(
-                        source.at[there], rows.at[spot(k, g, core, mine)],
-                        swap_send, swap_recv.at[k, core], (node, target),
-                    )
-
-    acc_in[...] = jnp.zeros_like(acc_in)
-    acc_out[...] = jnp.zeros_like(acc_out)
+    def swap(k, flip):
+        target = turn(x, SIDE - DX[k]) * CORES + lax.rem(core + flip, CORES)
+        there = pl.ds(pl.multiple_of(target * CAP, CAP), CAP)
+        mine = jnp.where(core == 0, block(0, 0, 0), block(1, 0, 0))
+        for g, source in enumerate((out_x, out_g)):
+            push(
+                source.at[there], rows.at[spot(k, g, core, mine)],
+                swap_send, swap_recv.at[k, core], (node, target),
+            )
 
     def ship(k, g, part, place, device, event):
         where = rows.at[spot(k, g, part, place)]
         push(where, where, gather_send.at[k], gather_recv.at[k, part, event], device)
 
-    def gather_start(k, first=False):
-        for part in range(CORES):
-            if first:
-                pl.when(core != part)(lambda: drain(rows, 2 * CAP, swap_recv.at[k, part]))
-            else:
-                drain(rows, 2 * CAP, swap_recv.at[k, part])
-            for g in range(2):
-                mine = block(part, 0, 0)
-                ship(k, g, part, mine, on_primary(part, 1), 0)
-                ship(k, g, part, mine, on_primary(part, 3), 1)
-            for g in range(2):
-                ship(k, g, part, mine, on_secondary(part, 1), 3)
-                ship(k, g, part, mine, on_secondary(part, 3), 4)
+    def gather_own(k, part):
+        mine = block(part, 0, 0)
+        for g in range(2):
+            ship(k, g, part, mine, on_primary(part, 1), 0)
+            ship(k, g, part, mine, on_primary(part, 3), 1)
+        for g in range(2):
+            ship(k, g, part, mine, on_secondary(part, 1), 3)
+            ship(k, g, part, mine, on_secondary(part, 3), 4)
+
+    def gather_start(k):
+        for part in range(CORES):
+            drain(rows, 2 * CAP, swap_recv.at[k, part])
+            gather_own(k, part)
 
     def gather_near(k):
         for part in range(CORES):
@@ -191,10 +190,13 @@
         start = ((k * 2 + g) * 2 + part) * PART
         return pl.ds(pl.multiple_of(start, PART), PART)
 
+    def span_of(k, part):
+        return pl.ds(pl.multiple_of(k * CHUNK + part * PART, PART), PART)
+
     def activate(k, part):
         pre = jnp.dot(rows[section(k, 0, part), :], w1[...], preferred_element_type=F32)
         activated, slope = gelu_parts(pre)
-        hidden_t[:, part * PART : (part + 1) * PART] = activated.T.astype(BF16)
+        hidden_t[:, span_of(k, part)] = activated.T.astype(BF16)
         slopes[part * PART : (part + 1) * PART, :] = slope
 
     def backward(k, part):
@@ -205,69 +207,79 @@
         )
         change = back_hidden * slopes[span, :]
         delta[span, :] = change.astype(BF16)
-        delta_t[:, span] = change.T.astype(BF16)
+        delta_t[:, span_of(k, part)] = change.T.astype(BF16)
 
     def to_inputs(k, part):
         span = slice(part * PART, (part + 1) * PART)
         for start in range(0, width, units):
-            back[
-                pl.ds(pl.multiple_of(k * CHUNK + part * PART, PART), PART), start : start + units
-            ] = lax.dot_general(
+            back[span_of(k, part), start : start + units] = lax.dot_general(
                 delta[span, :], w1[start : start + units, :], (((1,), (1,)), ((), ())),
                 preferred_element_type=F32,
             ).astype(BF16)
 
-    def to_weights(k, g, left, total, start):
-        span = pl.ds(pl.multiple_of((k * 2 + g) * CHUNK, CHUNK), CHUNK)
-        total[:, start : start + units] += jnp.dot(
-            left[...], rows[span, start : start + units], preferred_element_type=F32
-        )
-
     def pieces(k):
-        done = []
-        for part in range(CORES):
-            done.append(functools.partial(activate, k, part))
-        for part in range(CORES):
-            done.append(functools.partial(backward, k, part))
-        for part in range(CORES):
-            done.append(functools.partial(to_inputs, k, part))
-        for g, left, total in ((1, hidden_t, acc_out), (0, delta_t, acc_in)):
-            for start in range(0, width, units):
-                done.append(functools.partial(to_weights, k, g, left, total, start))
-        return done
+        return [
+            functools.partial(piece, k, part)
+            for piece in (activate, backward, to_inputs)
+            for part in range(CORES)
+        ]
+
+    def product(left, g, start):
+        total = None
+        for k in range(CHUNKS):
+            term = jnp.dot(
+                left[:, k * CHUNK : (k + 1) * CHUNK],
+                rows[pl.ds((k * 2 + g) * CHUNK, CHUNK), start : start + units],
+                preferred_element_type=F32,
+            )
+            total = term if total is None else total + term
+        return total
+
+    def second_weights(start):
+        rounded[:, start : start + units] = product(hidden_t, 1, start).astype(BF16)
+
+    def first_weights(start):
+        turned[start : start + units, :] = product(delta_t, 0, start).T.astype(BF16)
 
     def run(work, count):
         for _ in range(min(count, len(work))):
             work.pop(0)()
 
-    gather_start(0, first=True)
+    swap(0, 1)
+    for part in range(CORES):
+        pl.when(core == part)(functools.partial(gather_own, 0, part))
+    for k in range(1, CHUNKS):
+        for flip in range(CORES):
+            swap(k, flip)
+    for part in range(CORES):
+
+        @pl.when(core != part)
+        def _():
+            drain(rows, 2 * CAP, swap_recv.at[0, part])
+            gather_own(0, part)
+
     first_load.wait()
     second_load.wait()
 
     @pl.loop(0, CHUNKS)
     def _(k):
-        def compute(count):
-            @pl.when(k > 0)
-            def _():
-                run(work, count)
-
         work = pieces(k - 1)
+
+        def after_first(step):
+            pl.when(k > 0)(step)
+
         gather_near(k)
-        compute(3)
+        after_first(lambda: gather_pass(k - 1, 7, (2,)))
+        pl.when(k < CHUNKS - 1)(lambda: gather_start(k + 1))
         gather_pass(k, 3, (0,))
-        compute(2)
+        after_first(lambda: gather_end(k - 1))
+        after_first(lambda: run(work, 2))
         gather_far(k)
-
-        @pl.when(k < CHUNKS - 1)
-        def _():
-            gather_start(k + 1)
-
-        compute(3)
+        after_first(lambda: run(work, 2))
         gather_pass(k, 5, (3, 1))
-        compute(3)
-        gather_pass(k, 7, (2,))
-        compute(3)
-        gather_end(k)
+        after_first(lambda: run(work, 2))
+
+    gather_pass(CHUNKS - 1, 7, (2,))
 
     def strip(k, part, db, low, high):
         start = k * CHUNK + part * PART + turn(secondary[part], db) * COLUMN + low
@@ -311,16 +323,19 @@
 
     lanes = (pl.ds(0, half), pl.ds(half, half))
 
+    def column_add(k, part):
+        drain(back, COLUMN, sum_recv.at[k, part, 2])
+        drain(back, COLUMN, sum_recv.at[k, part, 3])
+        where = strip(k, part, 0, 0, COLUMN)
+        back[where, :] = (
+            back[where, :].astype(F32)
+            + arrived[k, part, 0].astype(F32)
+            + arrived[k, part, 1].astype(F32)
+        ).astype(BF16)
+
     def column_end(k):
         for part in range(CORES):
-            drain(back, COLUMN, sum_recv.at[k, part, 2])
-            drain(back, COLUMN, sum_recv.at[k, part, 3])
-            where = strip(k, part, 0, 0, COLUMN)
-            back[where, :] = (
-                back[where, :].astype(F32)
-                + arrived[k, part, 0].astype(F32)
-                + arrived[k, part, 1].astype(F32)
-            ).astype(BF16)
+            column_add(k, part)
             for side, step in ((0, 1), (1, 3)):
                 push(
                     back.at[lump(k, part, 2), lanes[side]], relay_block.at[k, part, side],
@@ -330,6 +345,19 @@
                 push(
                     back.at[lump(k, part, step), lanes[1 - side]],
                     arrived_block.at[k, part, side, :, lanes[1 - side]],
+                    sum_send.at[k], sum_recv.at[k, part, 6 + side], on_primary(part, step),
+                )
+
+    def column_last(k):
+        for part in range(CORES):
+            column_add(k, part)
+            push(
+                back.at[lump(k, part, 2)], across.at[part],
+                sum_send.at[k], sum_recv.at[k, part, 4], on_primary(part, 2),
+            )
+            for side, step in ((0, 1), (1, 3)):
+                push(
+                    back.at[lump(k, part, step)], arrived_block.at[k, part, side],
                     sum_send.at[k], sum_recv.at[k, part, 6 + side], on_primary(part, step),
                 )
 
@@ -349,7 +377,7 @@
                     sum_send.at[k], sum_recv.at[k, part, 6 + side], on_primary(part, step),
                 )
 
-    def block_end(k):
+    def block_end(k, direct=False):
         for part in range(CORES):
             drain(back, CAP, sum_recv.at[k, part, 6])
             drain(back, CAP, sum_recv.at[k, part, 7])
@@ -357,7 +385,11 @@
                 back[lump(k, part, 0), :].astype(F32)
                 + arrived_block[k, part, 0].astype(F32)
                 + arrived_block[k, part, 1].astype(F32)
-            ).astype(BF16)
+            )
+            if direct:
+                drain(back, CAP, sum_recv.at[k, part, 4])
+                total = total + across[part].astype(F32)
+            total = total.astype(BF16)
             target = (node, turn(x, DX[k]) * CORES + part)
 
             def keep():
@@ -377,40 +409,45 @@
                 send()
 
     work = pieces(CHUNKS - 1)
-    r0, r1, r2, r3 = RETURN_ORDER
-    column_start(r0)
-    column_start(r1)
+    column_start(1)
+    column_start(2)
+    column_start(0)
+    gather_end(CHUNKS - 1)
     run(work, 2)
-    column_pass(r0)
+    column_pass(1)
     run(work, 2)
-    column_pass(r1)
+    column_pass(2)
     run(work, 2)
-    column_end(r0)
-    column_start(r2)
-    run(work, 2)
-    column_end(r1)
-    block_pass(r0)
-    run(work, 2)
-    column_pass(r2)
-    column_start(r3)
-    run(work, 2)
-    block_end(r0)
-    block_pass(r1)
-    run(work, 2)
-    first_store = pltpu.make_async_copy(acc_out, grad_second.at[0], store_sem.at[0])
-    first_store.start()
-    column_end(r2)
-    column_pass(r3)
-    block_end(r1)
-    block_pass(r2)
-    for start in range(0, width, units):
-        acc_turned[start : start + units, :] = acc_in[:, start : start + units].T
-    second_store = pltpu.make_async_copy(acc_turned, grad_in.at[0], store_sem.at[1])
-    second_store.start()
-    column_end(r3)
-    block_end(r2)
-    block_pass(r3)
-    block_end(r3)
+    column_start(3)
+    column_end(1)
+    column_pass(0)
+    second_weights(0 * units)
+    block_pass(1)
+    column_end(2)
+    second_weights(1 * units)
+    column_pass(3)
+    block_end(1)
+    block_pass(2)
+    column_end(0)
+    second_weights(2 * units)
+    block_end(2)
+    block_pass(0)
+    second_weights(3 * units)
+    column_last(3)
+    first_weights(0 * units)
+    first_weights(1 * units)
+    block_end(0)
+    first_weights(2 * units)
+    first_weights(3 * units)
+    stores = [
+        pltpu.make_async_copy(ref, out, store_sem.at[i])
+        for i, (ref, out) in enumerate(
+            ((rounded, grad_second), (turned, grad_in), (held, picked_out))
+        )
+    ]
+    for store in stores:
+        store.start()
+    block_end(3, direct=True)
 
     for k in range(CHUNKS):
         for part in range(CORES):
@@ -418,17 +455,56 @@
                 drain(back, CAP, home_recv.at[k, part])
             else:
                 pl.when(core != part)(lambda: drain(back, CAP, home_recv.at[k, part]))
-    grad_tokens[...] = jnp.dot(
-        held[...], returned[...], preferred_element_type=F32
-    ).astype(BF16)
-
-    first_store.wait()
-    second_store.wait()
+    last = pltpu.make_async_copy(returned, returned_out, store_sem.at[3])
+    last.start()
     drain(rows, 2 * (EXPERTS - 1) * CAP, swap_send)
     drain(rows, (EXPERTS - 1) * CAP, home_send)
     for k in range(CHUNKS):
         drain(rows, CORES * 30 * CAP, gather_send.at[k])
-        drain(rows, CORES * 15 * CAP, sum_send.at[k])
+        drain(rows, CORES * (15 if k != RETURN_ORDER[-1] else 15) * CAP, sum_send.at[k])
+    for store in stores:
+        store.wait()
+    last.wait()
+
+
+def finish(
+    picked, returned, turned, rounded,
+    grad_tokens, grad_in, grad_second,
+    from_first, from_second, to_first, to_second, rows, held, total, load_sem, store_sem,
+):
+    loads, stores = [], []
+    for source, near in ((picked, held), (returned, rows)):
+        loads.append(pltpu.make_async_copy(source, near, load_sem.at[len(loads)]))
+    for source, near in ((turned, from_first), (rounded, from_second)):
+        height = source.shape[0] // PIECES
+        for piece in range(PIECES):
+            span = pl.ds(piece * height, height)
+            loads.append(
+                pltpu.make_async_copy(source.at[span], near.at[span], load_sem.at[len(loads)])
+            )
+    for load in loads:
+        load.start()
+
+    def store(near, target):
+        stores.append(pltpu.make_async_copy(near, target, store_sem.at[len(stores)]))
+        stores[-1].start()
+
+    for load in loads[:2]:
+        load.wait()
+    total[...] = jnp.dot(held[...], rows[...], preferred_element_type=F32).astype(BF16)
+    store(total, grad_tokens)
+    arrivals = iter(loads[2:])
+    for near, wide, target in (
+        (from_first, to_first, grad_in), (from_second, to_second, grad_second),
+    ):
+        height = near.shape[0] // PIECES
+        for piece in range(PIECES):
+            span = pl.ds(piece * height, height)
+            next(arrivals).wait()
+            wide[span, :] = near[span, :].astype(F32)
+            store(wide.at[span], target.at[0, span])
+    for started in stores:
+        started.wait()
 
 
 def body(tokens, grad_out, gate_weights, expert_ids, slot_ids, counts, w_in, w_out):
@@ -437,38 +513,40 @@
     in_vmem = pl.BlockSpec(memory_space=pltpu.VMEM)
     in_hbm = pl.BlockSpec(memory_space=pl.ANY)
     dma = pltpu.SemaphoreType.DMA
-    return pl.pallas_call(
+    slots = EXPERTS * CAP
+    results = pl.pallas_call(
         kernel,
         out_shape=(
-            jax.ShapeDtypeStruct(tokens.shape, BF16),
-            jax.ShapeDtypeStruct(w_in.shape, F32),
-            jax.ShapeDtypeStruct(w_out.shape, F32),
+            jax.ShapeDtypeStruct((token_rows, slots), BF16),
+            jax.ShapeDtypeStruct((slots, width), BF16),
+            jax.ShapeDtypeStruct((width, units), BF16),
+            jax.ShapeDtypeStruct((units, width), BF16),
         ),
         in_specs=[in_vmem] * 6 + [in_hbm] * 2,
-        out_specs=(in_vmem, in_hbm, in_hbm),
+        out_specs=(in_hbm,) * 4,
         scratch_shapes=[
             pltpu.VMEM((CHUNKS * 2 * CHUNK, width), BF16),
             pltpu.VMEM((width, units), BF16),
             pltpu.VMEM((units, width), BF16),
             pltpu.VMEM((CHUNKS * CHUNK, width), BF16),
-            pltpu.VMEM((units, width), F32),
-            pltpu.VMEM((units, width), F32),
-            pltpu.VMEM((width, units), F32),
+            pltpu.VMEM((width, units), BF16),
+            pltpu.VMEM((units, width), BF16),
             pltpu.VMEM((EXPERTS * CAP, width), BF16),
             pltpu.VMEM((EXPERTS * CAP, width), BF16),
             pltpu.VMEM((EXPERTS * CAP, width), BF16),
             pltpu.VMEM((token_rows, EXPERTS * CAP), BF16),
-            pltpu.VMEM((units, CHUNK), BF16),
+            pltpu.VMEM((units, CHUNKS * CHUNK), BF16),
             pltpu.VMEM((CHUNK, units), BF16),
-            pltpu.VMEM((units, CHUNK), BF16),
+            pltpu.VMEM((units, CHUNKS * CHUNK), BF16),
             pltpu.VMEM((CHUNK, units), F32),
             pltpu.VMEM((CHUNKS, CORES, 2, COLUMN // 2, width), BF16),
             pltpu.VMEM((CHUNKS, CORES, 2, COLUMN, width), BF16),
             pltpu.VMEM((CHUNKS, CORES, 2, CAP, width // 2), BF16),
             pltpu.VMEM((CHUNKS, CORES, 2, CAP, width), BF16),
+            pltpu.VMEM((CORES, CAP, width), BF16),
             pltpu.VMEM((CHUNKS, CORES, CAP, width), BF16),
             dma((2,)),
-            dma((2,)),
+            dma((4,)),
             dma,
             dma((CHUNKS, CORES)),
             dma((CHUNKS,)),
@@ -486,7 +564,29 @@
             bytes_accessed=16 * width * units,
             transcendentals=0,
         ),
-    )(tokens, grad_out, gate_weights, expert_ids, slot_ids, counts, w_in, w_out)
+    )(tokens, grad_out, gate_weights.T, expert_ids.T, slot_ids.T, counts, w_in, w_out)
+    return pl.pallas_call(
+        finish,
+        out_shape=(
+            jax.ShapeDtypeStruct(tokens.shape, BF16),
+            jax.ShapeDtypeStruct(w_in.shape, F32),
+            jax.ShapeDtypeStruct(w_out.shape, F32),
+        ),
+        in_specs=[in_hbm] * 4,
+        out_specs=(in_hbm,) * 3,
+        scratch_shapes=[
+            pltpu.VMEM((width, units), BF16),
+            pltpu.VMEM((units, width), BF16),
+            pltpu.VMEM((width, units), F32),
+            pltpu.VMEM((units, width), F32),
+            pltpu.VMEM((slots, width), BF16),
+            pltpu.VMEM((token_rows, slots), BF16),
+            pltpu.VMEM((token_rows, width), BF16),
+            dma((2 + 2 * PIECES,)),
+            dma((1 + 2 * PIECES,)),
+        ],
+        compiler_params=pltpu.CompilerParams(vmem_limit_bytes=62 * 2**20),
+    )(*results)
 
 
 def solution(mesh):

time: 171 us -> 157 us (0.918)
  local copies, waits for them, and re-layouts: 13 us -> 0 us
    unnamed x8 -> x0, local copies, waits for them, and re-layouts: 13 us -> none
    pallas_call x1 -> x2, Pallas kernels: 157 us -> 156 us  [the longest x1 152 us: body(): pl.pallas_call(kernel, out_shape=(jax.ShapeDtypeStruct((token_rows, slots...]
where the time goes in v2:
time: 157 us
  Pallas kernels  156 us (99%)
    pallas_call x1, Pallas kernels, body(): pl.pallas_call(kernel, out_shape=(jax.ShapeDtypeStruct((token_rows, slots...  152 us
    pallas_call x1, Pallas kernels, body(): pl.pallas_call(finish, out_shape=(jax.ShapeDtypeStruct(tokens.shape, BF16...  4.98 us

profile of v2, /device:TPU:1, one launch (start us, length us, event | category | flops | bytes accessed | tf_op | source)
XLA Modules:
  0.0 157.3 jit_solution(3823937180892731398)
XLA Ops:
  0.6 151.5 %shard_map.103 = (bf16[128,128]{1,0:T(8,128)(2,1)}, bf16[128,2048]{1,0:T(8,128)(2,1)}, bf16[2048,512]{1,0:T(8,128)(2,1)}, bf16[512,2048]{1,0:T(8,128)(2,1)}) custom-call(bf16[128,2048]{1,0:T(8,128)(2,1)} %tokens.1, bf16[128,2048]{1,0:T(8,128)(2,1)} %grad_out.1, f32[2,128]{1,0:T(2,128)} %bitcast.3, s32[2,128]{1,0:T(2,128)} %bitcast.4, s32[2,128]{1,0:T(2,128)} %bitcast.5, ...), custom_call_target="tpu_custom_call" | custom-call | flops 21474836480 | bytes 16777216 | tf_op jit(solution)/shard_map/pallas_call | solution.py:517
  152.1 5.0 %shard_map.104 = (bf16[128,2048]{1,0:T(8,128)(2,1)}, f32[1,2048,512]{2,1,0:T(8,128)}, f32[1,512,2048]{2,1,0:T(8,128)}) custom-call(bf16[128,128]{1,0:T(8,128)(2,1)} %get-tuple-element.7.picked, bf16[128,2048]{1,0:T(8,128)(2,1)} %get-tuple-element.8.returned, bf16[2048,512]{1,0:T(8,128)(2,1)} %get-tuple-element.9.turned, ...), custom_call_target="tpu_custom_call" | custom-call | tf_op jit(solution)/shard_map/pallas_call | solution.py:568

commit v3 on v0

v3 whole, which is shorter than its diff:
```python
import functools

import jax
import jax.numpy as jnp
from jax import lax
from jax.experimental import pallas as pl
from jax.experimental.pallas import tpu as pltpu
from jax.sharding import PartitionSpec as P

MESH = pl.DeviceIdType.MESH
BF16 = jnp.bfloat16
F32 = jnp.float32

SIDE = 4
CORES = 2
EXPERTS = 8
CAP = 16
NODES = SIDE * SIDE
CHUNKS = SIDE
DX = (0, 1, 3, 2)
PAIR = 2 * CAP
PART = NODES * CAP
CHUNK = CORES * PART
PIECES = 4
TILES = 4


def gelu_parts(values):
    cumulative = 0.5 * (1.0 + lax.erf(values * 0.7071067811865476))
    density = values * jnp.exp(-0.5 * values * values) * 0.3989422804014327
    return (values * cumulative, cumulative + density)


def turn(value, step):
    return lax.rem(value + step, SIDE)


def kernel(
    tokens, grad_out, gates, ids, slots, counts, w_in, w_out,
    picked_out, returned_out, grad_in, grad_second,
    rows, w1, w2, back, other_core, turned, rounded, out_x, out_g, returned, held,
    hidden_t, delta, delta_t, slopes, sum_a, sum_b, sum_c, sum_d, sum_e, final,
    weight_send, weight_recv, store_sem, swap_send, swap_recv,
    gather_send, gather_recv, core_send, core_recv,
    add_send, add_recv, sum_send, sum_recv, grad_send, grad_recv, home_send, home_recv,
):
    width = rows.shape[1]
    units = w2.shape[0]
    tile = width // TILES
    node, local = lax.axis_index("node"), lax.axis_index("local")
    y, z = node // SIDE, lax.rem(node, SIDE)
    x, core = local // CORES, lax.rem(local, CORES)

    side = lax.rem((y + 1) // 2, 2)
    half_y = y // 2
    mate_y = y + 1 - 2 * lax.rem(y, 2)
    guest = core != side

    def turn(value, step):
        return lax.rem(value + step, SIDE)

    sibling = (node, x * CORES + 1 - core)
    across = ((SIDE - 1 - y) * SIDE + z, local)
    above = (y * SIDE + turn(z, 1), local)
    below = (y * SIDE + turn(z, 3), local)
    trade = (mate_y * SIDE + z, x * CORES + 1 - core)

    def peer(mate, step):
        there = mate_y if mate else y
        return (there * SIDE + z, turn(x, step) * CORES + core)

    def spot(k, g, low_y, at_z, count):
        start = ((k * 2 + g) * 2 + core) * PART + (at_z * SIDE + low_y) * CAP
        return pl.ds(pl.multiple_of(start, CAP), count)

    def block(k, g, other, dz):
        half = 1 - half_y if other else half_y
        return rows.at[spot(k, g, 2 * half, turn(z, dz), PAIR)]

    def settle(ref, sem):
        pltpu.make_async_copy(ref, ref, sem).wait()

    def drain(ref, count, sem):
        settle(ref.at[pl.ds(0, count)], sem)

    def push(src, dst, send, recv, device):
        pltpu.make_async_remote_copy(
            src_ref=src, dst_ref=dst, send_sem=send, recv_sem=recv,
            device_id=device, device_id_type=MESH,
        ).start()

    barrier = pltpu.get_barrier_semaphore()
    partners = [sibling, across, above, below, trade]
    for step in range(SIDE):
        for mate in (False, True):
            if step or mate:
                partners.append(peer(mate, step))
    for partner in partners:
        pl.semaphore_signal(barrier, inc=1, device_id=partner, device_id_type=MESH)

    @pl.when(jnp.logical_not(guest))
    def _():
        pltpu.make_async_copy(w_in.at[0], w1, weight_recv.at[0]).start()
        pltpu.make_async_copy(w_out.at[0], w2, weight_recv.at[1]).start()

    limits = counts[...].astype(F32)
    expert_lanes = lax.broadcasted_iota(jnp.int32, (ids.shape[1], EXPERTS), 1)
    slot_lanes = lax.broadcasted_iota(jnp.int32, (ids.shape[1], EXPERTS * CAP), 1)
    picks, weighted = None, None
    ids_down, slots_down, gates_down = (
        jnp.concatenate([ref[...].astype(F32)] * 4, axis=0).T for ref in (ids, slots, gates)
    )
    for choice in range(2):
        expert = ids_down[:, choice : choice + 1].astype(jnp.int32)
        slot = slots_down[:, choice : choice + 1].astype(jnp.int32)
        limit = jnp.sum(
            jnp.where(expert == expert_lanes, limits, 0.0), axis=1, keepdims=True
        )
        place = jnp.where(slot.astype(F32) < limit, expert * CAP + slot, -1)
        pick = jnp.where(place == slot_lanes, 1.0, 0.0)
        scale = pick * gates_down[:, choice : choice + 1]
        picks = pick if picks is None else picks + pick
        weighted = scale if weighted is None else weighted + scale
    held[...] = picks.astype(BF16)
    to_slots = picks.T.astype(BF16)
    slot_gate = jnp.sum(weighted.T, axis=1, keepdims=True)
    out_x[...] = jnp.dot(to_slots, tokens[...], preferred_element_type=F32).astype(BF16)
    out_g[...] = (
        slot_gate * jnp.dot(to_slots, grad_out[...], preferred_element_type=F32)
    ).astype(BF16)
    def slots_of(expert):
        return pl.ds(pl.multiple_of(expert * CAP, CAP), CAP)

    served = x * CORES + side
    for g, source in enumerate((out_x, out_g)):
        rows[spot(0, g, y, z, CAP), :] = source[slots_of(served), :]

    pl.semaphore_wait(barrier, len(partners))

    def swap(k, mate):
        target = peer(mate, SIDE - DX[k])
        there = turn(x, SIDE - DX[k]) * CORES + (1 - side if mate else side)
        for g, source in enumerate((out_x, out_g)):
            push(
                source.at[slots_of(there)], rows.at[spot(k, g, y, z, CAP)],
                swap_send, swap_recv.at[k, int(mate)], target,
            )

    def ship(k, g, other, dz, device, event):
        where = block(k, g, other, dz)
        push(where, where, gather_send.at[k], gather_recv.at[k, event], device)

    def share(k, g, other, dz):
        where = block(k, g, other, dz)
        push(where, where, core_send.at[k], core_recv.at[k], sibling)

    def gather_start(k, first=False):
        if not first:
            drain(rows, 2 * CAP, swap_recv.at[k, 0])
        drain(rows, 2 * CAP, swap_recv.at[k, 1])
        for g in range(2):
            ship(k, g, False, 0, across, 0)
            ship(k, g, False, 0, above, 1)
            ship(k, g, False, 0, below, 2)
        for g in range(2):
            share(k, g, False, 0)

    def gather_cross(k):
        drain(rows, 2 * PAIR, gather_recv.at[k, 0])
        for g in range(2):
            ship(k, g, True, 0, above, 4)
            ship(k, g, True, 0, below, 5)
        for g in range(2):
            share(k, g, True, 0)

    def gather_pass(k):
        drain(rows, 2 * PAIR, gather_recv.at[k, 1])
        ship(k, 0, False, 3, above, 3)
        drain(rows, 2 * PAIR, gather_recv.at[k, 2])
        ship(k, 1, False, 1, below, 3)
        for g in range(2):
            share(k, g, False, 3)
            share(k, g, False, 1)

    def gather_far(k):
        drain(rows, 2 * PAIR, gather_recv.at[k, 3])
        for g in range(2):
            ship(k, g, False, 2, across, 6)
        for g in range(2):
            share(k, g, False, 2)

    def gather_end(k):
        for event, dz in ((4, 3), (5, 1), (6, 2)):
            drain(rows, 2 * PAIR, gather_recv.at[k, event])
            for g in range(2):
                share(k, g, True, dz)

    def gather_done(k):
        drain(rows, 2 * PART, core_recv.at[k])

    def section(k, g, part):
        start = ((k * 2 + g) * 2 + part) * PART
        return pl.ds(pl.multiple_of(start, PART), PART)

    def span_of(k, part):
        return pl.ds(pl.multiple_of(k * CHUNK + part * PART, PART), PART)

    def activate(k, part):
        pre = jnp.dot(rows[section(k, 0, part), :], w1[...], preferred_element_type=F32)
        activated, slope = gelu_parts(pre)
        hidden_t[:, span_of(k, part)] = activated.T.astype(BF16)
        slopes[span_of(k, part), :] = slope

    def backward(k, part):
        span = span_of(k, part)
        back_hidden = lax.dot_general(
            rows[section(k, 1, part), :], w2[...], (((1,), (1,)), ((), ())),
            preferred_element_type=F32,
        )
        change = back_hidden * slopes[span, :]
        delta[span, :] = change.astype(BF16)
        delta_t[:, span] = change.T.astype(BF16)

    def both(step, k):
        for part in range(CORES):
            step(k, part)

    def to_inputs(k, part):
        span = span_of(k, part)
        for start in range(0, width, units):
            back[span, start : start + units] = lax.dot_general(
                delta[span, :], w1[start : start + units, :], (((1,), (1,)), ((), ())),
                preferred_element_type=F32,
            ).astype(BF16)

    def product(left, g, start):
        total = None
        for k in range(CHUNKS):
            term = jnp.dot(
                left[:, k * CHUNK : (k + 1) * CHUNK],
                rows[pl.ds((k * 2 + g) * CHUNK, CHUNK), start : start + units],
                preferred_element_type=F32,
            )
            total = term if total is None else total + term
        return total

    def settle_grad(ref, target, index):
        @pl.when(guest)
        def _():
            push(ref, target, grad_send.at[index], grad_recv.at[index], trade)

        @pl.when(jnp.logical_not(guest))
        def _():
            pltpu.make_async_copy(ref, target, grad_recv.at[index]).start()

    def second_weights(index):
        columns = pl.ds(index * tile, tile)
        rounded[:, columns] = product(hidden_t, 1, index * tile).astype(BF16)
        settle_grad(rounded.at[:, columns], grad_second.at[:, columns], 0)

    def first_weights(index):
        span = pl.ds(index * tile, tile)
        turned[span, :] = product(delta_t, 0, index * tile).T.astype(BF16)
        settle_grad(turned.at[span], grad_in.at[span], 1)

    def add_start(k):
        to_inputs(k, 1 - core)
        push(
            back.at[span_of(k, 1 - core)], other_core.at[k],
            add_send.at[k], add_recv.at[k], sibling,
        )
        to_inputs(k, core)

    def lump(k, other, dz, first=0, count=PAIR):
        half = 1 - half_y if other else half_y
        start = k * CHUNK + core * PART + (turn(z, dz) * SIDE + 2 * half) * CAP + first
        return pl.ds(pl.multiple_of(start, CAP), count)

    def add(where, *terms):
        total = back[where, :].astype(F32)
        for term in terms:
            total = total + term.astype(F32)
        back[where, :] = total.astype(BF16)

    def forward(k, where, target, event, device):
        push(back.at[where], target, sum_send.at[k], sum_recv.at[k, event], device)

    def sum_start(k):
        settle(other_core.at[k], add_recv.at[k])
        add(span_of(k, core), other_core[k])
        forward(k, lump(k, True, 2), sum_a.at[k], 0, across)
        forward(k, lump(k, True, 1), sum_b.at[k, 0], 1, above)
        forward(k, lump(k, True, 3), sum_b.at[k, 1], 2, below)
        forward(k, lump(k, False, 1, CAP, CAP), sum_e.at[k, 0, pl.ds(CAP, CAP)], 6, above)
        forward(k, lump(k, False, 3, 0, CAP), sum_e.at[k, 1, pl.ds(0, CAP)], 7, below)

    def sum_far(k):
        settle(sum_a.at[k], sum_recv.at[k, 0])
        add(lump(k, False, 2), sum_a[k])
        forward(k, lump(k, False, 2, 0, CAP), sum_c.at[k, 0], 3, above)
        forward(k, lump(k, False, 2, CAP, CAP), sum_c.at[k, 1], 4, below)

    def sum_cross(k):
        settle(sum_b.at[k, 0], sum_recv.at[k, 1])
        settle(sum_b.at[k, 1], sum_recv.at[k, 2])
        add(lump(k, True, 0), sum_b[k, 0], sum_b[k, 1])
        forward(k, lump(k, True, 0), sum_d.at[k], 5, across)

    def sum_pass(k):
        settle(sum_c.at[k, 0], sum_recv.at[k, 3])
        add(lump(k, False, 1, 0, CAP), sum_c[k, 0])
        forward(k, lump(k, False, 1, 0, CAP), sum_e.at[k, 0, pl.ds(0, CAP)], 6, above)
        settle(sum_c.at[k, 1], sum_recv.at[k, 4])
        add(lump(k, False, 3, CAP, CAP), sum_c[k, 1])
        forward(k, lump(k, False, 3, CAP, CAP), sum_e.at[k, 1, pl.ds(CAP, CAP)], 7, below)

    def sum_end(k):
        settle(sum_d.at[k], sum_recv.at[k, 5])
        settle(sum_e.at[k, 0], sum_recv.at[k, 6])
        settle(sum_e.at[k, 1], sum_recv.at[k, 7])
        final[k] = (
            back[lump(k, False, 0), :].astype(F32) + sum_d[k].astype(F32)
            + sum_e[k, 0].astype(F32) + sum_e[k, 1].astype(F32)
        ).astype(BF16)
        mine = pl.ds(pl.multiple_of((y - 2 * half_y) * CAP, CAP), CAP)
        mates = pl.ds(pl.multiple_of((mate_y - 2 * half_y) * CAP, CAP), CAP)
        if k == 0:
            returned[slots_of(served), :] = final[k, mine, :]
        else:
            push(
                final.at[k, mine], returned.at[slots_of(served)],
                home_send, home_recv.at[k, 0], peer(False, DX[k]),
            )
        push(
            final.at[k, mates], returned.at[slots_of(served)],
            home_send, home_recv.at[k, 1], peer(True, DX[k]),
        )

    swap(0, True)
    gather_start(0, first=True)
    swap(1, True)
    swap(1, False)

    @pl.when(guest)
    def _():
        push(w_in.at[0], w1, weight_send.at[0], weight_recv.at[0], trade)
        push(w_out.at[0], w2, weight_send.at[1], weight_recv.at[1], trade)

    gather_pass(0)
    gather_cross(0)
    gather_start(1)
    swap(2, True)
    swap(2, False)
    gather_far(0)
    swap(3, True)
    swap(3, False)
    gather_start(2)
    gather_pass(1)
    gather_cross(1)
    gather_far(1)
    gather_end(0)
    gather_start(3)
    gather_pass(2)
    gather_cross(2)
    gather_far(2)
    gather_end(1)
    first = pltpu.make_async_copy(held, picked_out, store_sem.at[0])
    first.start()
    settle(w1, weight_recv.at[0])
    gather_done(0)
    both(activate, 0)
    gather_pass(3)
    gather_cross(3)
    gather_done(1)
    both(activate, 1)
    gather_far(3)
    gather_end(2)
    gather_done(2)
    both(activate, 2)
    settle(w2, weight_recv.at[1])
    both(backward, 0)
    both(backward, 1)
    gather_end(3)
    both(backward, 2)
    gather_done(3)
    both(activate, 3)
    both(backward, 3)
    second_weights(0)
    add_start(0)
    second_weights(1)
    sum_start(0)
    add_start(1)
    second_weights(2)
    sum_far(0)
    sum_cross(0)
    sum_start(1)
    add_start(2)
    second_weights(3)
    sum_pass(0)
    sum_far(1)
    sum_cross(1)
    first_weights(0)
    sum_start(2)
    add_start(3)
    sum_end(0)
    first_weights(1)
    sum_pass(1)
    sum_far(2)
    sum_cross(2)
    first_weights(2)
    sum_start(3)
    sum_end(1)
    first_weights(3)
    sum_pass(2)
    sum_far(3)
    sum_cross(3)
    sum_end(2)
    sum_pass(3)
    sum_end(3)

    for k in range(CHUNKS):
        if k:
            drain(returned, CAP, home_recv.at[k, 0])
        drain(returned, CAP, home_recv.at[k, 1])
    last = pltpu.make_async_copy(returned, returned_out, store_sem.at[1])
    last.start()
    settle(grad_second, grad_recv.at[0])
    settle(grad_in, grad_recv.at[1])

    @pl.when(guest)
    def _():
        settle(w1, weight_send.at[0])
        settle(w2, weight_send.at[1])
        settle(grad_second, grad_send.at[0])
        settle(grad_in, grad_send.at[1])

    drain(rows, 2 * (2 * SIDE - 1) * CAP, swap_send)
    drain(rows, (2 * SIDE - 1) * CAP, home_send)
    for k in range(CHUNKS):
        drain(rows, 14 * PAIR, gather_send.at[k])
        drain(rows, 2 * PART, core_send.at[k])
        drain(rows, PART, add_send.at[k])
        drain(rows, 7 * PAIR, sum_send.at[k])
    first.wait()
    last.wait()


def finish(
    picked, returned, turned, rounded,
    grad_tokens, grad_in, grad_second,
    from_first, from_second, to_first, to_second, rows, held, total, load_sem, store_sem,
):
    loads, stores = [], []
    for source, near in ((picked, held), (returned, rows)):
        loads.append(pltpu.make_async_copy(source, near, load_sem.at[len(loads)]))
    for source, near in ((turned, from_first), (rounded, from_second)):
        height = source.shape[0] // PIECES
        for piece in range(PIECES):
            span = pl.ds(piece * height, height)
            loads.append(
                pltpu.make_async_copy(source.at[span], near.at[span], load_sem.at[len(loads)])
            )
    for load in loads:
        load.start()

    def store(near, target):
        stores.append(pltpu.make_async_copy(near, target, store_sem.at[len(stores)]))
        stores[-1].start()

    for load in loads[:2]:
        load.wait()
    total[...] = jnp.dot(held[...], rows[...], preferred_element_type=F32).astype(BF16)
    store(total, grad_tokens)
    arrivals = iter(loads[2:])
    for near, wide, target in (
        (from_first, to_first, grad_in), (from_second, to_second, grad_second),
    ):
        height = near.shape[0] // PIECES
        for piece in range(PIECES):
            span = pl.ds(piece * height, height)
            next(arrivals).wait()
            wide[span, :] = near[span, :].astype(F32)
            store(wide.at[span], target.at[0, span])
    for started in stores:
        started.wait()


def body(tokens, grad_out, gate_weights, expert_ids, slot_ids, counts, w_in, w_out):
    token_rows, width = tokens.shape
    units = w_out.shape[1]
    in_vmem = pl.BlockSpec(memory_space=pltpu.VMEM)
    in_hbm = pl.BlockSpec(memory_space=pl.ANY)
    dma = pltpu.SemaphoreType.DMA
    slots = EXPERTS * CAP
    results = pl.pallas_call(
        kernel,
        out_shape=(
            jax.ShapeDtypeStruct((token_rows, slots), BF16),
            jax.ShapeDtypeStruct((slots, width), BF16),
            jax.ShapeDtypeStruct((width, units), BF16),
            jax.ShapeDtypeStruct((units, width), BF16),
        ),
        in_specs=[in_vmem] * 6 + [in_hbm] * 2,
        out_specs=(in_hbm,) * 4,
        scratch_shapes=[
            pltpu.VMEM((CHUNKS * 2 * CHUNK, width), BF16),
            pltpu.VMEM((width, units), BF16),
            pltpu.VMEM((units, width), BF16),
            pltpu.VMEM((CHUNKS * CHUNK, width), BF16),
            pltpu.VMEM((CHUNKS, PART, width), BF16),
            pltpu.VMEM((width, units), BF16),
            pltpu.VMEM((units, width), BF16),
            pltpu.VMEM((EXPERTS * CAP, width), BF16),
            pltpu.VMEM((EXPERTS * CAP, width), BF16),
            pltpu.VMEM((EXPERTS * CAP, width), BF16),
            pltpu.VMEM((token_rows, EXPERTS * CAP), BF16),
            pltpu.VMEM((units, CHUNKS * CHUNK), BF16),
            pltpu.VMEM((CHUNKS * CHUNK, units), BF16),
            pltpu.VMEM((units, CHUNKS * CHUNK), BF16),
            pltpu.VMEM((CHUNKS * CHUNK, units), F32),
            pltpu.VMEM((CHUNKS, PAIR, width), BF16),
            pltpu.VMEM((CHUNKS, 2, PAIR, width), BF16),
            pltpu.VMEM((CHUNKS, 2, CAP, width), BF16),
            pltpu.VMEM((CHUNKS, PAIR, width), BF16),
            pltpu.VMEM((CHUNKS, 2, PAIR, width), BF16),
            pltpu.VMEM((CHUNKS, PAIR, width), BF16),
            dma((2,)),
            dma((2,)),
            dma((2,)),
            dma,
            dma((CHUNKS, 2)),
            dma((CHUNKS,)),
            dma((CHUNKS, 7)),
            dma((CHUNKS,)),
            dma((CHUNKS,)),
            dma((CHUNKS,)),
            dma((CHUNKS,)),
            dma((CHUNKS,)),
            dma((CHUNKS, 8)),
            dma((2,)),
            dma((2,)),
            dma,
            dma((CHUNKS, 2)),
        ],
        compiler_params=pltpu.CompilerParams(
            collective_id=0, has_side_effects=True, vmem_limit_bytes=62 * 2**20
        ),
        cost_estimate=pl.CostEstimate(
            flops=10 * NODES * EXPERTS * CAP * width * units,
            bytes_accessed=16 * width * units,
            transcendentals=0,
        ),
    )(tokens, grad_out, gate_weights.T, expert_ids.T, slot_ids.T, counts, w_in, w_out)
    return pl.pallas_call(
        finish,
        out_shape=(
            jax.ShapeDtypeStruct(tokens.shape, BF16),
            jax.ShapeDtypeStruct(w_in.shape, F32),
            jax.ShapeDtypeStruct(w_out.shape, F32),
        ),
        in_specs=[in_hbm] * 4,
        out_specs=(in_hbm,) * 3,
        scratch_shapes=[
            pltpu.VMEM((width, units), BF16),
            pltpu.VMEM((units, width), BF16),
            pltpu.VMEM((width, units), F32),
            pltpu.VMEM((units, width), F32),
            pltpu.VMEM((slots, width), BF16),
            pltpu.VMEM((token_rows, slots), BF16),
            pltpu.VMEM((token_rows, width), BF16),
            dma((2 + 2 * PIECES,)),
            dma((1 + 2 * PIECES,)),
        ],
        compiler_params=pltpu.CompilerParams(vmem_limit_bytes=62 * 2**20),
    )(*results)


def solution(mesh):
    placed = (
        P(("node", "local"), None),
        P(("node", "local"), None),
        P(("node", "local"), None),
        P(("node", "local"), None),
        P(("node", "local"), None),
        P(("node", "local"), None),
        P("local", None, "node"),
        P("local", "node", None),
    )
    return jax.shard_map(
        body,
        mesh=mesh,
        in_specs=placed,
        out_specs=(P(("node", "local"), None), P("local", None, "node"), P("local", "node", None)),
        check_vma=False,
    )
```

time: 338 us -> 140 us (0.41)
  waiting for transfers between devices: 210 us -> 0 us
  Pallas kernels: 0 us -> 139 us
  matrix products: 49 us -> 0 us
  blocking collectives: 28.5 us -> 0 us
  local copies, waits for them, and re-layouts: 19.3 us -> 0 us
  between operations: 13.9 us -> 0.8 us
  other arithmetic: 11.2 us -> 0 us
  starting transfers between devices: 5.67 us -> 0 us
    pallas_call x0 -> x2, Pallas kernels: none -> 139 us  [the longest x1 134 us: body(): pl.pallas_call(kernel, out_shape=(jax.ShapeDtypeStruct((token_rows, slots...]
    all_gather x2 -> x0, waiting for transfers between devices: 111 us -> none  [the longest x1 63.1 us: body(): grad_piece = lax.all_gather(received[1][None], 'node', axis=0, tiled=True)]
    reduce_scatter x1 -> x0, waiting for transfers between devices: 98.9 us -> none  [body(): lax.psum_scatter(lax.dot_general(all_deltas, w_first, (((1,), (1,)), ((),...]
    dot_general x5 -> x0, matrix products: 49 us -> none  [the longest x1 11.3 us: body(): lax.dot_general(hidden, grad_rows, (((0,), (0,)), ((), ())), preferred_el...]
    all_to_all x2 -> x0, blocking collectives: 28.5 us -> none  [the longest x1 15.1 us: body(): lax.all_to_all(input_buffer, 'local', split_axis=0, concat_axis=0, tiled=...]
    mul x3 -> x0, local copies, waits for them, and re-layouts: 7.2 us -> none  [body(): gate_weights[:, :, None] * grad_out[:, None, :].astype(jnp.float32)]
    all_to_all x1 -> x0, starting transfers between devices: 5.37 us -> none  [body(): lax.all_to_all(shares, 'local', split_axis=0, concat_axis=0, tiled=True)]
    reduce_sum x2 -> x0, other arithmetic: 5.07 us -> none  [the longest x1 4.15 us: body(): grad_tokens = jnp.sum(picked, axis=1).astype(jnp.bfloat16)]
  transfers between devices with their start and end apart: 4 -> 0, of which waited for: 3 -> 0; matrix products, arithmetic and copies ran while one was open for 13% -> 0% of each run, Pallas kernels for 0% -> 0%
where the time goes in v3:
time: 140 us
  Pallas kernels  139 us (99%)
    pallas_call x1, Pallas kernels, body(): pl.pallas_call(kernel, out_shape=(jax.ShapeDtypeStruct((token_rows, slots...  134 us
    pallas_call x1, Pallas kernels, body(): pl.pallas_call(finish, out_shape=(jax.ShapeDtypeStruct(tokens.shape, BF16...  4.98 us

profile of v3, /device:TPU:1, one launch (start us, length us, event | category | flops | bytes accessed | tf_op | source)
XLA Modules:
  0.0 139.7 jit_solution(17541469949914023734)
XLA Ops:
  0.6 133.9 %shard_map.103 = (bf16[128,128]{1,0:T(8,128)(2,1)}, bf16[128,2048]{1,0:T(8,128)(2,1)}, bf16[2048,512]{1,0:T(8,128)(2,1)}, bf16[512,2048]{1,0:T(8,128)(2,1)}) custom-call(bf16[128,2048]{1,0:T(8,128)(2,1)} %tokens.1, bf16[128,2048]{1,0:T(8,128)(2,1)} %grad_out.1, f32[2,128]{1,0:T(2,128)} %bitcast.3, s32[2,128]{1,0:T(2,128)} %bitcast.4, s32[2,128]{1,0:T(2,128)} %bitcast.5, ...), custom_call_target="tpu_custom_call" | custom-call | flops 21474836480 | bytes 16777216 | tf_op jit(solution)/shard_map/pallas_call | solution.py:495
  134.6 5.0 %shard_map.104 = (bf16[128,2048]{1,0:T(8,128)(2,1)}, f32[1,2048,512]{2,1,0:T(8,128)}, f32[1,512,2048]{2,1,0:T(8,128)}) custom-call(bf16[128,128]{1,0:T(8,128)(2,1)} %get-tuple-element.7.picked, bf16[128,2048]{1,0:T(8,128)(2,1)} %get-tuple-element.8.returned, bf16[2048,512]{1,0:T(8,128)(2,1)} %get-tuple-element.9.turned, ...), custom_call_target="tpu_custom_call" | custom-call | tf_op jit(solution)/shard_map/pallas_call | solution.py:554

commit v4 on v3

--- a/solution.py
+++ b/solution.py
@@ -154,16 +154,28 @@
         where = block(k, g, other, dz)
         push(where, where, core_send.at[k], core_recv.at[k], sibling)
 
-    def gather_start(k, first=False):
-        if not first:
-            drain(rows, 2 * CAP, swap_recv.at[k, 0])
-        drain(rows, 2 * CAP, swap_recv.at[k, 1])
+    def gather_first(from_y):
+        for g in range(2):
+            where = rows.at[spot(0, g, from_y, z, CAP)]
+            for event, device in enumerate((across, above, below)):
+                push(where, where, gather_send.at[0], gather_recv.at[0, event], device)
+        for g in range(2):
+            where = rows.at[spot(0, g, from_y, z, CAP)]
+            push(where, where, core_send.at[0], core_recv.at[0], sibling)
+
+    def gather_start(k):
+        for mate in range(2):
+            drain(rows, 2 * CAP, swap_recv.at[k, mate])
         for g in range(2):
             ship(k, g, False, 0, across, 0)
             ship(k, g, False, 0, above, 1)
             ship(k, g, False, 0, below, 2)
         for g in range(2):
             share(k, g, False, 0)
+
+    def gather_mate():
+        drain(rows, 2 * CAP, swap_recv.at[0, 1])
+        gather_first(mate_y)
 
     def gather_cross(k):
         drain(rows, 2 * PAIR, gather_recv.at[k, 0])
@@ -224,6 +236,10 @@
     def both(step, k):
         for part in range(CORES):
             step(k, part)
+
+    def slopes_of(k, part):
+        activate(k, part)
+        backward(k, part)
 
     def to_inputs(k, part):
         span = span_of(k, part)
@@ -337,7 +353,8 @@
         )
 
     swap(0, True)
-    gather_start(0, first=True)
+    gather_first(y)
+    gather_mate()
     swap(1, True)
     swap(1, False)
 
@@ -357,9 +374,9 @@
     gather_start(2)
     gather_pass(1)
     gather_cross(1)
+    gather_start(3)
     gather_far(1)
     gather_end(0)
-    gather_start(3)
     gather_pass(2)
     gather_cross(2)
     gather_far(2)
@@ -380,11 +397,11 @@
     settle(w2, weight_recv.at[1])
     both(backward, 0)
     both(backward, 1)
+    both(backward, 2)
     gather_end(3)
-    both(backward, 2)
+    slopes_of(3, core)
     gather_done(3)
-    both(activate, 3)
-    both(backward, 3)
+    slopes_of(3, 1 - core)
     second_weights(0)
     add_start(0)
     second_weights(1)
@@ -396,21 +413,21 @@
     sum_start(1)
     add_start(2)
     second_weights(3)
+    first_weights(0)
     sum_pass(0)
     sum_far(1)
     sum_cross(1)
-    first_weights(0)
     sum_start(2)
     add_start(3)
+    first_weights(1)
     sum_end(0)
-    first_weights(1)
     sum_pass(1)
     sum_far(2)
     sum_cross(2)
     first_weights(2)
     sum_start(3)
+    first_weights(3)
     sum_end(1)
-    first_weights(3)
     sum_pass(2)
     sum_far(3)
     sum_cross(3)

time: 140 us -> 137 us (0.979)
  Pallas kernels: 139 us -> 137 us
    pallas_call x1, Pallas kernels: 134 us -> 132 us  [body(): pl.pallas_call(kernel, out_shape=(jax.ShapeDtypeStruct((token_rows, slots...]
where the time goes in v4:
time: 137 us
  Pallas kernels  137 us (100%)
    pallas_call x1, Pallas kernels, body(): pl.pallas_call(kernel, out_shape=(jax.ShapeDtypeStruct((token_rows, slots...  132 us
    pallas_call x1, Pallas kernels, body(): pl.pallas_call(finish, out_shape=(jax.ShapeDtypeStruct(tokens.shape, BF16...  4.98 us

profile of v4, /device:TPU:1, one launch (start us, length us, event | category | flops | bytes accessed | tf_op | source)
XLA Modules:
  0.0 137.3 jit_solution(3589868750180430174)
XLA Ops:
  0.6 131.5 %shard_map.103 = (bf16[128,128]{1,0:T(8,128)(2,1)}, bf16[128,2048]{1,0:T(8,128)(2,1)}, bf16[2048,512]{1,0:T(8,128)(2,1)}, bf16[512,2048]{1,0:T(8,128)(2,1)}) custom-call(bf16[128,2048]{1,0:T(8,128)(2,1)} %tokens.1, bf16[128,2048]{1,0:T(8,128)(2,1)} %grad_out.1, f32[2,128]{1,0:T(2,128)} %bitcast.3, s32[2,128]{1,0:T(2,128)} %bitcast.4, s32[2,128]{1,0:T(2,128)} %bitcast.5, ...), custom_call_target="tpu_custom_call" | custom-call | flops 21474836480 | bytes 16777216 | tf_op jit(solution)/shard_map/pallas_call | solution.py:512
  132.2 5.0 %shard_map.104 = (bf16[128,2048]{1,0:T(8,128)(2,1)}, f32[1,2048,512]{2,1,0:T(8,128)}, f32[1,512,2048]{2,1,0:T(8,128)}) custom-call(bf16[128,128]{1,0:T(8,128)(2,1)} %get-tuple-element.7.picked, bf16[128,2048]{1,0:T(8,128)(2,1)} %get-tuple-element.8.returned, bf16[2048,512]{1,0:T(8,128)(2,1)} %get-tuple-element.9.turned, ...), custom_call_target="tpu_custom_call" | custom-call | tf_op jit(solution)/shard_map/pallas_call | solution.py:571

commit v5 on v4

--- a/solution.py
+++ b/solution.py
@@ -39,7 +39,7 @@
     tokens, grad_out, gates, ids, slots, counts, w_in, w_out,
     picked_out, returned_out, grad_in, grad_second,
     rows, w1, w2, back, other_core, turned, rounded, out_x, out_g, returned, held,
-    hidden_t, delta, delta_t, slopes, sum_a, sum_b, sum_c, sum_d, sum_e, final,
+    hidden_t, delta, delta_t, slopes, sum_a, sum_b, sum_c, sum_d, sum_e, final, early,
     weight_send, weight_recv, store_sem, swap_send, swap_recv,
     gather_send, gather_recv, core_send, core_recv,
     add_send, add_recv, sum_send, sum_recv, grad_send, grad_recv, home_send, home_recv,
@@ -249,12 +249,12 @@
                 preferred_element_type=F32,
             ).astype(BF16)
 
-    def product(left, g, start):
+    def product(left, g, start, chunks):
         total = None
-        for k in range(CHUNKS):
+        for k in chunks:
             term = jnp.dot(
                 left[:, k * CHUNK : (k + 1) * CHUNK],
-                rows[pl.ds((k * 2 + g) * CHUNK, CHUNK), start : start + units],
+                rows[pl.ds((k * 2 + g) * CHUNK, CHUNK), start : start + tile],
                 preferred_element_type=F32,
             )
             total = term if total is None else total + term
@@ -271,12 +271,19 @@
 
     def second_weights(index):
         columns = pl.ds(index * tile, tile)
-        rounded[:, columns] = product(hidden_t, 1, index * tile).astype(BF16)
+        if index:
+            total = product(hidden_t, 1, index * tile, range(CHUNKS))
+        else:
+            total = early[...] + product(hidden_t, 1, 0, (CHUNKS - 1,))
+        rounded[:, columns] = total.astype(BF16)
         settle_grad(rounded.at[:, columns], grad_second.at[:, columns], 0)
+
+    def second_early():
+        early[...] = product(hidden_t, 1, 0, range(CHUNKS - 1))
 
     def first_weights(index):
         span = pl.ds(index * tile, tile)
-        turned[span, :] = product(delta_t, 0, index * tile).T.astype(BF16)
+        turned[span, :] = product(delta_t, 0, index * tile, range(CHUNKS)).T.astype(BF16)
         settle_grad(turned.at[span], grad_in.at[span], 1)
 
     def add_start(k):
@@ -394,15 +401,17 @@
     gather_end(2)
     gather_done(2)
     both(activate, 2)
+    second_early()
     settle(w2, weight_recv.at[1])
     both(backward, 0)
     both(backward, 1)
     both(backward, 2)
     gather_end(3)
-    slopes_of(3, core)
+    activate(3, core)
     gather_done(3)
-    slopes_of(3, 1 - core)
+    activate(3, 1 - core)
     second_weights(0)
+    both(backward, 3)
     add_start(0)
     second_weights(1)
     sum_start(0)
@@ -541,6 +550,7 @@
             pltpu.VMEM((CHUNKS, PAIR, width), BF16),
             pltpu.VMEM((CHUNKS, 2, PAIR, width), BF16),
             pltpu.VMEM((CHUNKS, PAIR, width), BF16),
+            pltpu.VMEM((units, width // TILES), F32),
             dma((2,)),
             dma((2,)),
             dma((2,)),

time: 137 us -> 137 us (level)
  no operation moved by 1% of the time
where the time goes in v5:
time: 137 us
  Pallas kernels  136 us (99%)
    pallas_call x1, Pallas kernels, body(): pl.pallas_call(kernel, out_shape=(jax.ShapeDtypeStruct((token_rows, slots...  131 us
    pallas_call x1, Pallas kernels, body(): pl.pallas_call(finish, out_shape=(jax.ShapeDtypeStruct(tokens.shape, BF16...  4.99 us

profile of v5, /device:TPU:1, one launch (start us, length us, event | category | flops | bytes accessed | tf_op | source)
XLA Modules:
  0.0 136.7 jit_solution(11664599240920946284)
XLA Ops:
  0.6 130.9 %shard_map.103 = (bf16[128,128]{1,0:T(8,128)(2,1)}, bf16[128,2048]{1,0:T(8,128)(2,1)}, bf16[2048,512]{1,0:T(8,128)(2,1)}, bf16[512,2048]{1,0:T(8,128)(2,1)}) custom-call(bf16[128,2048]{1,0:T(8,128)(2,1)} %tokens.1, bf16[128,2048]{1,0:T(8,128)(2,1)} %grad_out.1, f32[2,128]{1,0:T(2,128)} %bitcast.3, s32[2,128]{1,0:T(2,128)} %bitcast.4, s32[2,128]{1,0:T(2,128)} %bitcast.5, ...), custom_call_target="tpu_custom_call" | custom-call | flops 21474836480 | bytes 16777216 | tf_op jit(solution)/shard_map/pallas_call | solution.py:521
  131.6 5.0 %shard_map.104 = (bf16[128,2048]{1,0:T(8,128)(2,1)}, f32[1,2048,512]{2,1,0:T(8,128)}, f32[1,512,2048]{2,1,0:T(8,128)}) custom-call(bf16[128,128]{1,0:T(8,128)(2,1)} %get-tuple-element.7.picked, bf16[128,2048]{1,0:T(8,128)(2,1)} %get-tuple-element.8.returned, bf16[2048,512]{1,0:T(8,128)(2,1)} %get-tuple-element.9.turned, ...), custom_call_target="tpu_custom_call" | custom-call | tf_op jit(solution)/shard_map/pallas_call | solution.py:581
